TPU v7x, 32 devices: a whole 2x2x4 slice. The times are simulated.
32 devices in a mesh: groups: 2 (over y), mp: 4 (over x, core), dp: 4 (over z).
Axes of the slice: x: 2, y: 2, z: 4, core: 2. Of those that a mesh axis runs over, the one named last changes fastest.
Arguments:
- qkv: bfloat16 [3, 8192, 4096], P(None, ('groups', 'dp'), 'mp'), parts along dimension 1, may hold values from -6.5 to 6.5
- grad_out: float32 [8192, 6144], P(('groups', 'dp'), 'mp'), parts along dimension 0, may hold values from -6 to 6
- out_weight: bfloat16 [4096, 6144], P('mp', 'dp'), may hold values from -0.09375 to 0.09375
- segments: int32 [16, 512], P(('groups', 'dp')), parts along dimension 0, may hold values from 0 to 15, as said below
Outputs:
- grad_qkv: bfloat16 [3, 8192, 4096], P(None, ('groups', 'dp'), 'mp'), parts along dimension 1
- grad_weight: bfloat16 [8192, 6144], P(('groups', 'mp'), 'dp'), parts along dimension 0
There are 2 independent parts, one for each index of `groups`. A program takes and returns all parts, laid end to end along the dimension named above; an argument that names none is the same for every part. Nothing has to cross between parts.
Inputs may be any that keep to these rules, and one draw needn't show every extreme that they name: `segments`: along each packed sequence the image ids start at 0 and never fall; every image covers a run of even length that starts at an even position.
All inputs are finite; a program needn't handle non-finite values.
Results may differ from a plain program's by a relative error of at most 0.0075.
Values may be sent and summed in bfloat16 or wider, within the bound.
No kernel may reach another device: no remote copies, remote signals or barrier semaphores. Data moves between devices by JAX's collectives and lax.ppermute only.
A program may use at most 256 MiB of HBM per device.

v0:
```python
import math

import jax
import jax.numpy as jnp
from jax import lax
from jax.sharding import PartitionSpec as P

HD = 128
LEN = 512


def masked_softmax(scores, allowed):
    scores = jnp.where(allowed[None], scores, -jnp.inf)
    row_max = jnp.max(scores, axis=-1, keepdims=True)
    exponent = jnp.exp(scores - row_max)
    return exponent / jnp.sum(exponent, axis=-1, keepdims=True)


def shards(qkv, grad_out, out_weight, segments):
    tokens_here = qkv.shape[1]
    width = qkv.shape[2]
    heads = width // HD
    seq_count = tokens_here // LEN
    score_scale = 1.0 / math.sqrt(HD)
    shaped = qkv.reshape(3, seq_count, LEN, heads, HD)

    def forward(bundle):
        queries, keys, values, segment_ids = bundle
        allowed = segment_ids[:, None] == segment_ids[None, :]
        scores = (
            jnp.einsum("qhd,khd->hqk", queries, keys, preferred_element_type=jnp.float32)
            * score_scale
        )
        probability = masked_softmax(scores, allowed)
        weights = probability.astype(jnp.bfloat16)
        attended = jnp.einsum("hqk,khd->qhd", weights, values, preferred_element_type=jnp.float32)
        return (probability, attended.astype(jnp.bfloat16))

    probabilities, attended = lax.map(forward, (shaped[0], shaped[1], shaped[2], segments))
    attended_rows = attended.reshape(tokens_here, width)
    projection = lax.all_gather(out_weight, "dp", axis=1, tiled=True)
    grad_rows = grad_out.astype(jnp.bfloat16)
    piece = lax.all_gather(grad_rows, "mp", axis=1, tiled=True)
    grad_att = lax.dot_general(
        piece, projection, (((1,), (1,)), ((), ())), preferred_element_type=jnp.float32
    )
    block = lax.dot_general(
        attended_rows, piece, (((0,), (0,)), ((), ())), preferred_element_type=jnp.float32
    )
    grad_att_sum = grad_att
    grad_weight = lax.psum_scatter(block, "dp", scatter_dimension=1, tiled=True).astype(
        jnp.bfloat16
    )
    grad_heads = grad_att_sum.astype(jnp.bfloat16).reshape(seq_count, LEN, heads, HD)

    def backward(bundle):
        probability, queries, keys, values, segment_ids, grad_att = bundle
        weights = probability.astype(jnp.bfloat16)
        grad_probs = jnp.einsum(
            "qhd,khd->hqk", grad_att, values, preferred_element_type=jnp.float32
        )
        row_dot = jnp.sum(probability * grad_probs, axis=-1, keepdims=True)
        grad_scores = (probability * (grad_probs - row_dot) * score_scale).astype(jnp.bfloat16)
        grad_queries = jnp.einsum(
            "hqk,khd->qhd", grad_scores, keys, preferred_element_type=jnp.float32
        )
        grad_keys = jnp.einsum(
            "hqk,qhd->khd", grad_scores, queries, preferred_element_type=jnp.float32
        )
        grad_values = jnp.einsum(
            "hqk,qhd->khd", weights, grad_att, preferred_element_type=jnp.float32
        )
        return jnp.stack([grad_queries, grad_keys, grad_values]).astype(jnp.bfloat16)

    grads = lax.map(
        backward, (probabilities, shaped[0], shaped[1], shaped[2], segments, grad_heads)
    )
    grad_qkv = jnp.transpose(grads, (1, 0, 2, 3, 4)).reshape(3, tokens_here, width)
    return (grad_qkv, grad_weight)


def solution(mesh):
    return jax.shard_map(
        shards,
        mesh=mesh,
        in_specs=(
            P(None, ("groups", "dp"), "mp"),
            P(("groups", "dp"), "mp"),
            P("mp", "dp"),
            P(("groups", "dp"), None),
        ),
        out_specs=(P(None, ("groups", "dp"), "mp"), P(("groups", "mp"), "dp")),
        check_vma=False,
    )
```

profile of v0, /device:TPU:0, one launch (start us, length us, event | category | flops | bytes accessed | tf_op | source)
XLA Modules:
  0.0 743.2 jit_solution(3487450546257645821)
XLA Ops:
  7.2 4.8 convert_element_type.32
  12.9 4.4 slice_bitcast_fusion
  23.2 50.2 %while.22 = (s32[]{:T(128)}, f32[2,8,512,512]{2,3,1,0:T(8,128)}, bf16[2,512,8,128]{3,2,1,0:T(8,128)(2,1)}, s32[2,512]{1,0:T(2,128)S(1)}, bf16[2,512,8,128]{3,2,1...) while((s32[]{:T(128)}, f32[2,8,512,512]{2,3,1,0:T(8,128)}, ...), condition=%wide.region_3.4_spmd, body=%wide.region_0.3_spmd.sunk | while | flops 1093403136 | bytes 67689568 | solution.py:39
  28.2 5.6 fusion.57
  34.5 4.2 fusion.58
  40.5 8.2 %bitcast_dynamic-update-slice_fusion.2 = f32[2,8,512,512]{2,3,1,0:T(8,128)} fusion(f32[2,8,512,512]{2,3,1,0:T(8,128)} %get-tuple-element.258, s32[]{:T(128)} %get-tuple-element.257, f32[8,512,512]{1,2,0:T(8,128)} %get-tuple-element.235, f32[8,512]{1,0:T(8,128)S(1)} %get-tuple-element.236), kind=kLoop, calls=%fused_computation.1.clone.1 | loop fusion | flops 2097152 | bytes 16794112 | tf_op jit(solution)/shard_map/while/body/jit(dynamic_update_index_in_dim)/dynamic_update_slice | solution.py:39
  53.1 5.6 fusion.57
  59.3 4.1 fusion.58
  65.3 8.1 %bitcast_dynamic-update-slice_fusion.2 = f32[2,8,512,512]{2,3,1,0:T(8,128)} fusion(f32[2,8,512,512]{2,3,1,0:T(8,128)} %get-tuple-element.258, s32[]{:T(128)} %get-tuple-element.257, f32[8,512,512]{1,2,0:T(8,128)} %get-tuple-element.235, f32[8,512]{1,0:T(8,128)S(1)} %get-tuple-element.236), kind=kLoop, calls=%fused_computation.1.clone.1 | loop fusion | flops 2097152 | bytes 16794112 | tf_op jit(solution)/shard_map/while/body/jit(dynamic_update_index_in_dim)/dynamic_update_slice | solution.py:39
  73.4 23.6 %all-gather.3.cloned.1.call-done = bf16[1024,6144]{1,0:T(8,128)(2,1)} async-done(((bf16[1024,1536]{1,0:T(8,128)(2,1)}), bf16[1024,6144]{1,0:T(8,128)(2,1)}) %all-gather.3.cloned.1.call-update) | async-done | bytes 12582928 | tf_op jit(solution)/shard_map/all_gather | solution.py:43
  97.0 21.5 %fusion.31 = f32[1024,6144]{1,0:T(8,128)} fusion(bf16[1024,6144]{1,0:T(8,128)(2,1)} %all-gather.3.cloned.1.call-done, bf16[128,8,8,128]{3,2,1,0:T(8,128)(2,1)} %bitcast.145), kind=kOutput, calls=%fused_computation.51 | convolution fusion | flops 12884901888 | bytes 39845888 | tf_op jit(solution)/shard_map/dot_general | solution.py:47
  118.5 198.3 %all-gather.5.cloned.1.call-done = bf16[1024,6144]{1,0:T(8,128)(2,1)} async-done(((bf16[1024,1536]{1,0:T(8,128)(2,1)}), bf16[1024,6144]{1,0:T(8,128)(2,1)}) %all-gather.5.cloned.1.call-update) | async-done | bytes 12582928 | tf_op jit(solution)/shard_map/all_gather | solution.py:41
  316.8 17.5 %convert_bitcast_fusion = bf16[128,8,8,128]{3,1,2,0:T(8,128)(2,1)S(1)} fusion(bf16[1024,6144]{1,0:T(8,128)(2,1)} %all-gather.3.cloned.1.call-done, bf16[1024,6144]{1,0:T(8,128)(2,1)} %all-gather.5.cloned.1.call-done), kind=kOutput, calls=%fused_computation.54 | convolution fusion | flops 12885950464 | bytes 27262976 | tf_op jit(solution)/shard_map/dot_general | solution.py:44
  336.3 81.9 %while.23 = (s32[]{:T(128)}, bf16[2,3,512,8,128]{2,4,3,1,0:T(8,128)(2,1)}, bf16[2,512,8,128]{3,2,1,0:T(8,128)(2,1)}, f32[2,8,512,512]{2,3,1,0:T(8,128)}, bf16[2,...) while((s32[]{:T(128)}, ...), condition=%wide.region_6.7_spmd, body=%wide.region_4.6_spmd.sunk | while | flops 2705854976 | bytes 79693408 | solution.py:75
  340.6 8.9 %fusion.64 = f32[8,512,512]{1,2,0:T(8,128)} fusion(f32[2,8,512,512]{2,3,1,0:T(8,128)} %get-tuple-element.292, s32[]{:T(128)} %get-tuple-element.281, bf16[1,512,8,128]{3,2,1,0:T(8,128)(2,1)S(1)} %get-tuple-element.246, bf16[1,512,8,128]{3,2,1,0:T(8,128)(2,1)S(1)} %get-tuple-element.245), kind=kOutput, calls=%fused_computation.25.clone.1 | convolution fusion | flops 538972672 | bytes 18874880 | tf_op jit(solution)/shard_map/while/body/eval_jaxpr/sub | solution.py:63
  349.5 9.3 %fusion.65 = bf16[8,512,512]{1,2,0:T(8,128)(2,1)} fusion(f32[8,512,512]{1,2,0:T(8,128)} %fusion.64, f32[2,8,512,512]{2,3,1,0:T(8,128)} %get-tuple-element.292, s32[]{:T(128)} %get-tuple-element.281, bf16[1,512,8,128]{3,2,1,0:T(8,128)(2,1)S(1)} %get-tuple-element.246, bf16[1,512,8,128]{3,2,1,0:T(8,128)(2,1)S(1)} %get-tuple-element.245), kind=kOutput, calls=%fused_computation.30.clone.1 | convolution fusion | flops 545259520 | bytes 23068676 | tf_op jit(solution)/shard_map/while/body/eval_jaxpr/qhd,khd->hqk/dot_general | solution.py:59
  370.0 4.9 fusion.63
  381.2 9.0 %fusion.64 = f32[8,512,512]{1,2,0:T(8,128)} fusion(f32[2,8,512,512]{2,3,1,0:T(8,128)} %get-tuple-element.292, s32[]{:T(128)} %get-tuple-element.281, bf16[1,512,8,128]{3,2,1,0:T(8,128)(2,1)S(1)} %get-tuple-element.246, bf16[1,512,8,128]{3,2,1,0:T(8,128)(2,1)S(1)} %get-tuple-element.245), kind=kOutput, calls=%fused_computation.25.clone.1 | convolution fusion | flops 538972672 | bytes 18874880 | tf_op jit(solution)/shard_map/while/body/eval_jaxpr/sub | solution.py:63
  390.2 9.3 %fusion.65 = bf16[8,512,512]{1,2,0:T(8,128)(2,1)} fusion(f32[8,512,512]{1,2,0:T(8,128)} %fusion.64, f32[2,8,512,512]{2,3,1,0:T(8,128)} %get-tuple-element.292, s32[]{:T(128)} %get-tuple-element.281, bf16[1,512,8,128]{3,2,1,0:T(8,128)(2,1)S(1)} %get-tuple-element.246, bf16[1,512,8,128]{3,2,1,0:T(8,128)(2,1)S(1)} %get-tuple-element.245), kind=kOutput, calls=%fused_computation.30.clone.1 | convolution fusion | flops 545259520 | bytes 23068676 | tf_op jit(solution)/shard_map/while/body/eval_jaxpr/qhd,khd->hqk/dot_general | solution.py:59
  411.1 5.1 fusion.63
  418.2 9.0 %copy.28 = bf16[3,2,512,8,128]{4,3,2,1,0:T(8,128)(2,1)} copy(bf16[3,2,512,8,128]{2,4,3,0,1:T(8,128)(2,1)} %bitcast.143) | data formatting | bytes 12582912 | tf_op jit(solution)/shard_map/transpose | solution.py:78
  427.1 10.3 %reshape.103 = bf16[3,1024,1024]{2,1,0:T(8,128)(2,1)} reshape(bf16[3,2,512,8,128]{4,3,2,1,0:T(8,128)(2,1)} %copy.28) | data formatting | bytes 12582912 | tf_op jit(solution)/shard_map/reshape | solution.py:78
  437.4 294.4 %reduce-scatter.2.cloned.1.call-done = f32[1024,1536]{1,0:T(8,128)} async-done(((f32[1024,6144]{1,0:T(8,128)}), f32[1024,1536]{1,0:T(8,128)}) %reduce-scatter.2.cloned.1.call-update) | async-done | bytes 6291472 | tf_op jit(solution)/shard_map/reduce_scatter | solution.py:51
  731.8 4.8 convert_element_type.34
  (45 shorter events, 58.4 us)
Async XLA Ops:
  7.2 89.9 %all-gather.3.cloned.1.call-start = ((), (), s32[]{:S(2)}) async-start(), calls=%async_computation.1 | async-start | bytes 15728640 | tf_op jit(solution)/shard_map/all_gather | solution.py:43
  12.1 304.8 %all-gather.5.cloned.1.call-start = ((), (), s32[]{:S(2)}) async-start(), calls=%async_computation.2 | async-start | bytes 15728640 | tf_op jit(solution)/shard_map/all_gather | solution.py:41
  12.8 719.0 %reduce-scatter.2.cloned.1.call-start = ((), (), s32[]{:S(2)}) async-start(), calls=%async_computation.3 | async-start | bytes 31457280 | tf_op jit(solution)/shard_map/reduce_scatter | solution.py:51
  17.2 5.9 copy-start
Sparse Core Ops, SparseCore 0:
  12.2 84.7 all-gather.2
  98.6 218.2 all-gather.4
  319.2 412.5 reduce-scatter.1
where the time goes:
time: 745 us; the launch traced here: 743 us
  waiting for transfers between devices  517 us (69%)
  matrix products  111 us (15%)
  local copies, waits for them, and re-layouts  59.4 us (8%)
  other arithmetic  41.5 us (6%)
  between operations  13.8 us (2%)
    reduce_scatter x1, waiting for transfers between devices, shards(): lax.psum_scatter(block, 'dp', scatter_dimension=1, tiled=True)  294 us
    all_gather x1, waiting for transfers between devices, shards(): projection = lax.all_gather(out_weight, 'dp', axis=1, tiled=True)  198 us
    dynamic_slice x16, local copies, waits for them, and re-layouts, shards(): lax.map(forward, (shaped[0], shaped[1], shaped[2], segments))  24.3 us
    all_gather x1, waiting for transfers between devices, shards(): piece = lax.all_gather(grad_rows, 'mp', axis=1, tiled=True)  23.6 us
    dot_general x1, matrix products, shards(): lax.dot_general(attended_rows, piece, (((0,), (0,)), ((), ())), preferred...  21.5 us
    dot_general x2, matrix products, backward(): jnp.einsum('qhd,khd->hqk', grad_att, values, preferred_element_type=jnp.f...  18.7 us
    sub x2, matrix products, backward(): grad_probs - row_dot  17.9 us
    dot_general x1, matrix products, shards(): lax.dot_general(piece, projection, (((1,), (1,)), ((), ())), preferred_el...  17.5 us
  transfers between devices with their start and end apart: 3, of which 3 were waited for; matrix products, arithmetic and copies ran while one was open for 27% of the time, Pallas kernels for 0%

commit v1 on v0

v1 whole, which is shorter than its diff:
```python
import functools
import math

import jax
import jax.numpy as jnp
from jax import lax
from jax.experimental import pallas as pl
from jax.experimental.pallas import tpu as pltpu
from jax.sharding import PartitionSpec as P

HD = 128
LEN = 512
SCALE = 1.0 / math.sqrt(HD)
CHUNKS = 4
NT = (((1,), (1,)), ((), ()))
NN = (((1,), (0,)), ((), ()))
TN = (((0,), (0,)), ((), ()))


def dot(a, b, dims):
    return lax.dot_general(a, b, dims, preferred_element_type=jnp.float32)


def probabilities(queries, keys, allowed):
    scores = jnp.where(allowed, dot(queries, keys, NT) * SCALE, -jnp.inf)
    exponent = jnp.exp(scores - jnp.max(scores, axis=-1, keepdims=True))
    return exponent * (1.0 / jnp.sum(exponent, axis=-1, keepdims=True))


def forward_kernel(column_ids, row_ids, qkv, attended):
    allowed = column_ids[0] == row_ids[0]
    for head in range(attended.shape[1] // HD):
        cols = slice(head * HD, (head + 1) * HD)
        weights = probabilities(qkv[0, :, cols], qkv[1, :, cols], allowed).astype(jnp.bfloat16)
        attended[:, cols] = dot(weights, qkv[2, :, cols], NN).astype(jnp.bfloat16)


def backward_kernel(column_ids, row_ids, qkv, grad_att, grad_qkv):
    allowed = column_ids[0] == row_ids[0]
    for head in range(grad_att.shape[1] // HD):
        cols = slice(head * HD, (head + 1) * HD)
        queries, keys, values = qkv[0, :, cols], qkv[1, :, cols], qkv[2, :, cols]
        grads = grad_att[:, cols]
        probability = probabilities(queries, keys, allowed)
        grad_probs = dot(grads, values, NT)
        row_dot = jnp.sum(probability * grad_probs, axis=-1, keepdims=True)
        grad_scores = (probability * (grad_probs - row_dot) * SCALE).astype(jnp.bfloat16)
        weights = probability.astype(jnp.bfloat16)
        grad_qkv[0, :, cols] = dot(grad_scores, keys, NN).astype(jnp.bfloat16)
        grad_qkv[1, :, cols] = dot(grad_scores, queries, TN).astype(jnp.bfloat16)
        grad_qkv[2, :, cols] = dot(weights, grads, TN).astype(jnp.bfloat16)


def attention_call(kernel, segments, qkv, grad_att=None):
    tokens, width = qkv.shape[1:]
    seqs = tokens // LEN
    block = 2 * HD
    rows = pl.BlockSpec((LEN, block), lambda s, h: (s, h))
    three = pl.BlockSpec((3, LEN, block), lambda s, h: (0, s, h))
    in_specs = [
        pl.BlockSpec((1, LEN, 1), lambda s, h: (s, 0, 0)),
        pl.BlockSpec((1, 1, LEN), lambda s, h: (s, 0, 0)),
        three,
    ]
    operands = [segments.reshape(seqs, LEN, 1), segments.reshape(seqs, 1, LEN), qkv]
    out_specs, out_shape, products = rows, (tokens, width), 2
    if grad_att is not None:
        in_specs.append(rows)
        operands.append(grad_att)
        out_specs, out_shape, products = three, qkv.shape, 5
    return pl.pallas_call(
        kernel,
        grid=(seqs, width // block),
        in_specs=in_specs,
        out_specs=out_specs,
        out_shape=jax.ShapeDtypeStruct(out_shape, jnp.bfloat16),
        compiler_params=pltpu.CompilerParams(vmem_limit_bytes=48 * 2**20),
        cost_estimate=pl.CostEstimate(
            flops=2 * products * tokens * LEN * width,
            bytes_accessed=2 * products * 2 * tokens * width,
            transcendentals=tokens * LEN * width // HD,
        ),
    )(*operands)


def shards(groups, mp, dp, qkv, grad_out, out_weight, segments):
    tokens, width = qkv.shape[1:]
    own_width = grad_out.shape[1]
    per = mp // dp
    group = lax.axis_index("groups")
    here = lax.axis_index("mp")
    place = lax.axis_index("dp")

    def along(array, pairs):
        return lax.ppermute(array, "dp", pairs)

    def across_groups(array, shift, places):
        pairs = [
            (g * dp + k, (g + shift) % groups * dp + k) for g in range(groups) for k in places
        ]
        return lax.ppermute(array, ("groups", "dp"), pairs)

    with jax.named_scope("projection_along_dp"):
        part_rows = width // groups
        own_part = lax.dynamic_slice_in_dim(out_weight, group * part_rows, part_rows, 0)
        rights, lefts = [], []
        to_right = to_left = own_part
        for step in range(dp - 1):
            to_right = along(to_right, [(k, k + 1) for k in range(step, dp - 1)])
            to_left = along(to_left, [(k, k - 1) for k in range(1, dp - step)])
            rights.append(to_right)
            lefts.append(to_left)

    attended = attention_call(forward_kernel, segments, qkv)

    with jax.named_scope("output_gradient_over_mp"):
        chunk = own_width // CHUNKS
        gathered = []
        for c in range(CHUNKS):
            mine = grad_out[:, c * chunk : (c + 1) * chunk].astype(jnp.bfloat16)
            blocks = {0: mine}
            bit = mp // 2
            while bit:
                pairs = [(i, i ^ bit) for i in range(mp)]
                blocks |= {at | bit: lax.ppermute(b, "mp", pairs) for at, b in blocks.items()}
                bit //= 2
            gathered.append(jnp.stack([blocks[at] for at in range(mp)]))

    with jax.named_scope("weight_gradient_partials"):
        partials = [
            lax.dot_general(
                gathered[c],
                attended,
                (((1,), (0,)), ((), ())),
                preferred_element_type=jnp.float32,
            )
            for c in range(CHUNKS)
        ]

    def pick(stacked, which, axis):
        found = [
            lax.dynamic_index_in_dim(stacked, (which * per + j) ^ here, 0, keepdims=False)
            for j in range(per)
        ]
        return found[0] if per == 1 else jnp.concatenate(found, axis=axis)

    with jax.named_scope("weight_gradient_along_dp"):
        from_left = [None] * CHUNKS
        from_right = [None] * CHUNKS
        for step in range(dp - 1):
            for c in range(CHUNKS):
                right = pick(partials[c], jnp.minimum(dp - 1 - step + place, dp - 1), 0)
                left = pick(partials[c], jnp.maximum(step - dp + 1 + place, 0), 0)
                if step:
                    right = right + from_left[c].astype(jnp.float32)
                    left = left + from_right[c].astype(jnp.float32)
                from_left[c] = along(
                    right.astype(jnp.bfloat16),
                    [(k, k + 1) for k in range(min(step + 1, dp - 1))],
                )
                from_right[c] = along(
                    left.astype(jnp.bfloat16),
                    [(k, k - 1) for k in range(max(dp - 1 - step, 1), dp)],
                )
        sums = []
        for c in range(CHUNKS):
            total = pick(partials[c], place, 0)
            total = total + from_left[c].astype(jnp.float32) + from_right[c].astype(jnp.float32)
            sums.append(total.astype(jnp.bfloat16).T.reshape(width, per, chunk))
        grad_weight = jnp.stack(sums, axis=2).reshape(width, per * own_width)

    with jax.named_scope("attended_gradient"):
        whole = jnp.concatenate(gathered, axis=2)

        def product(which, parts):
            features = pick(whole, which, 1)
            return dot(features, jnp.concatenate(parts, axis=0), NT)

        own_parts = [
            lax.dynamic_slice_in_dim(
                out_weight, (group + j) % groups * part_rows, part_rows, 0
            )
            for j in range(groups)
        ]
        total = product(place, own_parts)
        for step in range(dp - 1):
            back = dp - 2 - step
            parts = [rights[step] + lefts[back]]
            for j in range(1, groups):
                parts.append(
                    across_groups(rights[step], -j, range(step + 1, dp))
                    + across_groups(lefts[back], -j, range(0, dp - 1 - back))
                )
            total = total + product((place - 1 - step) % dp, parts)
        rounded = total.astype(jnp.bfloat16)
        grad_att = jnp.roll(rounded, group * part_rows, axis=1)

    grad_qkv = attention_call(backward_kernel, segments, qkv, grad_att)
    return grad_qkv, grad_weight


def solution(mesh):
    body = functools.partial(shards, *(mesh.shape[name] for name in ("groups", "mp", "dp")))
    return jax.shard_map(
        body,
        mesh=mesh,
        in_specs=(
            P(None, ("groups", "dp"), "mp"),
            P(("groups", "dp"), "mp"),
            P("mp", "dp"),
            P(("groups", "dp"), None),
        ),
        out_specs=(P(None, ("groups", "dp"), "mp"), P(("groups", "mp"), "dp")),
        check_vma=False,
    )
```

time: 745 us -> 533 us (0.72)
  waiting for transfers between devices: 517 us -> 203 us
  starting transfers between devices: 0.12 us -> 138 us
  matrix products: 111 us -> 47.2 us
  local copies, waits for them, and re-layouts: 59.4 us -> 19.4 us
  other arithmetic: 41.5 us -> 79 us
  Pallas kernels: 0 us -> 35.1 us
  between operations: 13.8 us -> 2.1 us
    reduce_scatter x1 -> x0, waiting for transfers between devices: 294 us -> none  [shards(): lax.psum_scatter(block, 'dp', scatter_dimension=1, tiled=True)]
    all_gather x2 -> x0, waiting for transfers between devices: 222 us -> none  [the longest x1 198 us: shards(): projection = lax.all_gather(out_weight, 'dp', axis=1, tiled=True)]
    ppermute x0 -> x48, waiting for transfers between devices: none -> 203 us  [the longest x30 134 us: along(): return lax.ppermute(array, 'dp', pairs)]
    ppermute x0 -> x48, starting transfers between devices: none -> 138 us  [the longest x30 115 us: along(): return lax.ppermute(array, 'dp', pairs)]
    dot_general x14 -> x8, matrix products: 93.3 us -> 47.2 us  [the longest x4 29 us: dot(): return lax.dot_general(a, b, dims, preferred_element_type=jnp.float32)]
    pallas_call x0 -> x2, Pallas kernels: none -> 35.1 us  [attention_call(): pl.pallas_call(kernel, grid=(seqs, width // block), in_specs=in_specs, ou...]
    concatenate x0 -> x2, other arithmetic: none -> 26.5 us  [the longest x1 25.3 us: shards(): whole = jnp.concatenate(gathered, axis=2)]
    dynamic_slice x16 -> x1, local copies, waits for them, and re-layouts: 24.3 us -> 2.3 us  [shards(): lax.dynamic_slice_in_dim(out_weight, (group + j) % groups * part_rows, pa...]
  transfers between devices with their start and end apart: 3 -> 48, of which waited for: 3 -> 18; matrix products, arithmetic and copies ran while one was open for 27% -> 24% of each run, Pallas kernels for 0% -> 2%
where the time goes in v1:
time: 533 us; the launch traced here: 524 us
  waiting for transfers between devices  203 us (38%)
  starting transfers between devices  138 us (26%)
  other arithmetic  79 us (15%)
  matrix products  47.2 us (9%)
  Pallas kernels  35.1 us (7%)
  local copies, waits for them, and re-layouts  19.4 us (4%)
    ppermute x30, waiting for transfers between devices, along(): return lax.ppermute(array, 'dp', pairs)  134 us
    ppermute x30, starting transfers between devices, along(): return lax.ppermute(array, 'dp', pairs)  115 us
    ppermute x12, waiting for transfers between devices, shards(): lax.ppermute(b, 'mp', pairs)  42.4 us
    pallas_call x2, Pallas kernels, attention_call(): pl.pallas_call(kernel, grid=(seqs, width // block), in_specs=in_specs, ou...  35.1 us
    dot_general x4, matrix products, dot(): return lax.dot_general(a, b, dims, preferred_element_type=jnp.float32)  29 us
    ppermute x6, waiting for transfers between devices, across_groups(): return lax.ppermute(array, ('groups', 'dp'), pairs)  26.8 us
    concatenate x1, other arithmetic, shards(): whole = jnp.concatenate(gathered, axis=2)  25.3 us
    convert_element_type x8, other arithmetic, shards(): right.astype(jnp.bfloat16)  19.7 us
  transfers between devices with their start and end apart: 48, of which 18 were waited for; matrix products, arithmetic and copies ran while one was open for 24% of the time, Pallas kernels for 2%

profile of v1, /device:TPU:0, one launch (start us, length us, event | category | flops | bytes accessed | tf_op | source)
XLA Modules:
  0.0 524.0 jit_solution(10591903326898539071)
XLA Ops:
  15.0 16.7 %collective-permute-done.1 = bf16[1024,384]{0,1:T(8,128)(2,1)} collective-permute-done((bf16[1024,384]{0,1:T(8,128)(2,1)}, bf16[1024,384]{0,1:T(8,128)(2,1)}, u32[]{:S(2)}, u32[]{:S(2)}) %collective-permute-start.1) | collective-permute-done | bytes 786464 | tf_op jit(solution)/shard_map/output_gradient_over_mp/ppermute | solution.py:125
  32.4 12.7 %shard_map.60 = bf16[1024,1024]{1,0:T(8,128)(2,1)S(1)} custom-call(s32[2,512,1]{2,1,0:T(8,128)S(1)} %copy.17.column_ids, s32[2,1,512]{2,1,0:T(1,128)S(1)} %reshape.36.row_ids, bf16[3,1024,1024]{2,1,0:T(8,128)(2,1)} %qkv.3), custom_call_target="tpu_custom_call" | custom-call | flops 2147483648 | bytes 8388608 | tf_op jit(solution)/shard_map/pallas_call | solution.py:71
  50.6 14.8 %collective-permute-done.7 = bf16[1024,384]{0,1:T(8,128)(2,1)} collective-permute-done((bf16[1024,384]{0,1:T(8,128)(2,1)}, bf16[1024,384]{0,1:T(8,128)(2,1)}, u32[]{:S(2)}, u32[]{:S(2)}) %collective-permute-start.7) | collective-permute-done | bytes 786464 | tf_op jit(solution)/shard_map/output_gradient_over_mp/ppermute | solution.py:125
  71.3 10.0 %collective-permute-done.10 = bf16[1024,384]{0,1:T(8,128)(2,1)S(1)} collective-permute-done((bf16[1024,384]{0,1:T(8,128)(2,1)S(1)}, bf16[1024,384]{0,1:T(8,128)(2,1)S(1)}, u32[]{:S(2)}, u32[]{:S(2)}) %collective-permute-start.10) | collective-permute-done | bytes 786464 | tf_op jit(solution)/shard_map/output_gradient_over_mp/ppermute | solution.py:125
  135.1 10.6 %collective-permute-start.31 = (bf16[384,1024]{1,0:T(8,128)(2,1)}, bf16[384,1024]{1,0:T(8,128)(2,1)}, u32[]{:S(2)}, u32[]{:S(2)}) collective-permute-start(bf16[384,1024]{1,0:T(8,128)(2,1)} %fusion.75), channel_id=1, source_target_pairs={{0,1},{1,2},{4,5},{5,6},{8,9},{9,10},{12,13},{13,14},{16,17},{17,1... | collective-permute-start | bytes 2359304 | tf_op jit(solution)/shard_map/weight_gradient_along_dp/ppermute | solution.py:95
  146.6 17.1 %collective-permute-start.12 = (bf16[512,1536]{1,0:T(8,128)(2,1)}, bf16[512,1536]{1,0:T(8,128)(2,1)}, u32[]{:S(2)}, u32[]{:S(2)}) collective-permute-start(bf16[512,1536]{1,0:T(8,128)(2,1)} %get-tuple-element.23), channel_id=1, source_target_pairs={{0,1},{1,2},{2,3},{4,5},{5,6},{6,7},{8,9},{9,10},{10,11},{12,13},{... | collective-permute-start | bytes 4718600 | tf_op jit(solution)/shard_map/projection_along_dp/ppermute | solution.py:95
  170.9 6.8 %collective-permute-done.25 = bf16[384,1024]{1,0:T(8,128)(2,1)} collective-permute-done((bf16[384,1024]{1,0:T(8,128)(2,1)}, bf16[384,1024]{1,0:T(8,128)(2,1)}, u32[]{:S(2)}, u32[]{:S(2)}) %collective-permute-start.25) | collective-permute-done | bytes 786464 | tf_op jit(solution)/shard_map/weight_gradient_along_dp/ppermute | solution.py:95
  179.0 15.6 %collective-permute-done.31 = bf16[384,1024]{1,0:T(8,128)(2,1)} collective-permute-done((bf16[384,1024]{1,0:T(8,128)(2,1)}, bf16[384,1024]{1,0:T(8,128)(2,1)}, u32[]{:S(2)}, u32[]{:S(2)}) %collective-permute-start.31) | collective-permute-done | bytes 786464 | tf_op jit(solution)/shard_map/weight_gradient_along_dp/ppermute | solution.py:95
  206.4 38.7 %collective-permute-done.37 = bf16[384,1024]{1,0:T(8,128)(2,1)S(1)} collective-permute-done((bf16[384,1024]{1,0:T(8,128)(2,1)S(1)}, bf16[384,1024]{1,0:T(8,128)(2,1)S(1)}, u32[]{:S(2)}, u32[]{:S(2)}) %collective-permute-start.37) | collective-permute-done | bytes 786464 | tf_op jit(solution)/shard_map/weight_gradient_along_dp/ppermute | solution.py:95
  252.7 8.5 %collective-permute-done.43 = bf16[384,1024]{1,0:T(8,128)(2,1)} collective-permute-done((bf16[384,1024]{1,0:T(8,128)(2,1)S(1)}, bf16[384,1024]{1,0:T(8,128)(2,1)}, u32[]{:S(2)}, u32[]{:S(2)}) %collective-permute-start.43) | collective-permute-done | bytes 786464 | tf_op jit(solution)/shard_map/weight_gradient_along_dp/ppermute | solution.py:95
  274.4 14.6 %collective-permute-start.38 = (bf16[384,1024]{1,0:T(8,128)(2,1)}, bf16[384,1024]{1,0:T(8,128)(2,1)S(1)}, u32[]{:S(2)}, u32[]{:S(2)}) collective-permute-start(bf16[384,1024]{1,0:T(8,128)(2,1)} %get-tuple-element.14), channel_id=1, source_target_pairs={{0,1},{1,2},{2,3},{4,5},{5,6},{6,7},{8,9},{9,10},{10,11},{12,13},{... | collective-permute-start | bytes 2359304 | tf_op jit(solution)/shard_map/weight_gradient_along_dp/ppermute | solution.py:95
  298.9 14.6 %collective-permute-start.44 = (bf16[384,1024]{1,0:T(8,128)(2,1)}, bf16[384,1024]{1,0:T(8,128)(2,1)S(1)}, u32[]{:S(2)}, u32[]{:S(2)}) collective-permute-start(bf16[384,1024]{1,0:T(8,128)(2,1)} %get-tuple-element.18), channel_id=1, source_target_pairs={{0,1},{1,2},{2,3},{4,5},{5,6},{6,7},{8,9},{9,10},{10,11},{12,13},{... | collective-permute-start | bytes 2359304 | tf_op jit(solution)/shard_map/weight_gradient_along_dp/ppermute | solution.py:95
  316.2 7.8 %collective-permute-done.38 = bf16[384,1024]{1,0:T(8,128)(2,1)S(1)} collective-permute-done((bf16[384,1024]{1,0:T(8,128)(2,1)}, bf16[384,1024]{1,0:T(8,128)(2,1)S(1)}, u32[]{:S(2)}, u32[]{:S(2)}) %collective-permute-start.38) | collective-permute-done | bytes 786464 | tf_op jit(solution)/shard_map/weight_gradient_along_dp/ppermute | solution.py:95
  326.6 25.3 %maximum_maximum_fusion = bf16[4,1024,1536]{1,2,0:T(8,128)(2,1)} fusion(bf16[1,1024,384]{1,2,0:T(8,128)(2,1)S(1)} %bitcast.191, bf16[1,1024,384]{1,2,0:T(8,128)(2,1)S(1)} %bitcast.183, bf16[1,1024,384]{1,2,0:T(8,128)(2,1)S(1)} %bitcast.189, bf16[1,1024,384]{1,2,0:T(8,128)(2,1)S(1)} %copy-done.13, bf16[1,1024,384]{1,2,0:T(8,128)(2,1)S(1)} %bitcast.187, ...), kind=kLoop, calls=%fused_computation | loop fusion | flops 201326592 | bytes 25165824 | tf_op jit(solution)/shard_map/attended_gradient/concatenate | solution.py:173
  352.8 17.9 %collective-permute-done.29 = bf16[384,1024]{1,0:T(8,128)(2,1)} collective-permute-done((bf16[384,1024]{1,0:T(8,128)(2,1)}, bf16[384,1024]{1,0:T(8,128)(2,1)}, u32[]{:S(2)}, u32[]{:S(2)}) %collective-permute-start.29) | collective-permute-done | bytes 786464 | tf_op jit(solution)/shard_map/weight_gradient_along_dp/ppermute | solution.py:95
  373.9 13.6 %collective-permute-done.35 = bf16[384,1024]{1,0:T(8,128)(2,1)} collective-permute-done((bf16[384,1024]{1,0:T(8,128)(2,1)}, bf16[384,1024]{1,0:T(8,128)(2,1)}, u32[]{:S(2)}, u32[]{:S(2)}) %collective-permute-start.35) | collective-permute-done | bytes 786464 | tf_op jit(solution)/shard_map/weight_gradient_along_dp/ppermute | solution.py:95
  391.2 10.1 %collective-permute-done.41 = bf16[384,1024]{1,0:T(8,128)(2,1)} collective-permute-done((bf16[384,1024]{1,0:T(8,128)(2,1)}, bf16[384,1024]{1,0:T(8,128)(2,1)}, u32[]{:S(2)}, u32[]{:S(2)}) %collective-permute-start.41) | collective-permute-done | bytes 786464 | tf_op jit(solution)/shard_map/weight_gradient_along_dp/ppermute | solution.py:95
  402.6 7.8 %fusion.32 = f32[1024,1024]{1,0:T(8,128)} fusion(bf16[512,1536]{1,0:T(8,128)(2,1)S(1)} %copy-done.15, bf16[512,1536]{1,0:T(8,128)(2,1)S(1)} %copy-done.14, bf16[4,1024,1536]{1,2,0:T(8,128)(2,1)} %maximum_maximum_fusion, s32[]{:T(128)S(6)} %select_n.98), kind=kOutput, calls=%fused_computation.36 | convolution fusion | flops 3227516928 | bytes 10485764 | tf_op jit(solution)/shard_map/attended_gradient/dot_general | solution.py:21
  446.6 7.9 %fusion.40 = f32[1024,1024]{1,0:T(8,128)} fusion(bf16[512,1536]{1,0:T(8,128)(2,1)S(1)} %add.243, bf16[512,1536]{1,0:T(8,128)(2,1)S(1)} %copy-done.18, bf16[4,1024,1536]{1,2,0:T(8,128)(2,1)} %maximum_maximum_fusion, s32[]{:T(128)S(6)} %select_n.107), kind=kOutput, calls=%fused_computation.44 | convolution fusion | flops 3227516928 | bytes 10485764 | tf_op jit(solution)/shard_map/attended_gradient/dot_general | solution.py:21
  454.5 6.5 %collective-permute-done.17 = bf16[512,1536]{1,0:T(8,128)(2,1)} collective-permute-done((bf16[512,1536]{1,0:T(8,128)(2,1)}, bf16[512,1536]{1,0:T(8,128)(2,1)}, u32[]{:S(2)}, u32[]{:S(2)}) %collective-permute-start.17) | collective-permute-done | bytes 1572896 | tf_op jit(solution)/shard_map/attended_gradient/ppermute | solution.py:101
  463.3 6.2 %fusion.36 = f32[1024,1024]{1,0:T(8,128)} fusion(bf16[512,1536]{1,0:T(8,128)(2,1)S(1)} %add.238, bf16[512,1536]{1,0:T(8,128)(2,1)S(1)} %add.237, bf16[4,1024,1536]{1,2,0:T(8,128)(2,1)S(1)} %bitcast.178, s32[]{:T(128)S(6)} %select_n.104), kind=kOutput, calls=%fused_computation.40 | convolution fusion | flops 3227516928 | bytes 10485764 | tf_op jit(solution)/shard_map/attended_gradient/dot_general | solution.py:21
  469.5 20.3 %collective-permute-done.23 = bf16[512,1536]{1,0:T(8,128)(2,1)S(1)} collective-permute-done((bf16[512,1536]{1,0:T(8,128)(2,1)}, bf16[512,1536]{1,0:T(8,128)(2,1)S(1)}, u32[]{:S(2)}, u32[]{:S(2)}) %collective-permute-start.23) | collective-permute-done | bytes 1572896 | tf_op jit(solution)/shard_map/attended_gradient/ppermute | solution.py:101
  492.8 7.1 %add_convert_fusion = bf16[1024,1024]{1,0:T(8,128)(2,1)S(1)} fusion(f32[1024,1024]{1,0:T(8,128)} %fusion.40, f32[1024,1024]{1,0:T(8,128)} %fusion.32, f32[1024,1024]{1,0:T(8,128)} %fusion.36, bf16[512,1536]{1,0:T(8,128)(2,1)} %add.248, bf16[512,1536]{1,0:T(8,128)(2,1)S(1)} %add.247, bf16[4,1024,1536]{1,2,0:T(8,128)(2,1)S(1)} %bitcast.178, s32[]{:T(128)S(6)} %select_n.109), kind=kOutput, calls=%fused_computation.3 | convolution fusion | flops 3231711232 | bytes 20971524 | tf_op jit(solution)/shard_map/attended_gradient/dot_general | solution.py:21
  501.2 22.4 %shard_map.59 = bf16[3,1024,1024]{2,1,0:T(8,128)(2,1)} custom-call(s32[2,512,1]{2,1,0:T(8,128)S(1)} %copy.17.column_ids, s32[2,1,512]{2,1,0:T(1,128)S(1)} %reshape.36.row_ids, bf16[3,1024,1024]{2,1,0:T(8,128)(2,1)} %qkv.3, bf16[1024,1024]{1,0:T(8,128)(2,1)S(1)} %fusion.56.grad_att), custom_call_target="tpu_custom_call" | custom-call | flops 5368709120 | bytes 20971520 | tf_op jit(solution)/shard_map/pallas_call | solution.py:71
  (214 shorter events, 188.3 us)
Async XLA Ops:
  13.1 52.2 %collective-permute-start.7 = (bf16[1024,384]{0,1:T(8,128)(2,1)}, bf16[1024,384]{0,1:T(8,128)(2,1)}, u32[]{:S(2)}, u32[]{:S(2)}) collective-permute-start(bf16[1024,384]{0,1:T(8,128)(2,1)} %get-tuple-element.30), channel_id=1, source_target_pairs={{0,8},{4,12},{8,0},{12,4},{1,9},{5,13},{9,1},{13,5},{2,10},{6,14},... | collective-permute-start | bytes 2359304 | tf_op jit(solution)/shard_map/output_gradient_over_mp/ppermute | solution.py:125
  47.5 40.2 %collective-permute-start.6 = (bf16[1024,384]{0,1:T(8,128)(2,1)}, bf16[1024,384]{0,1:T(8,128)(2,1)S(1)}, u32[]{:S(2)}, u32[]{:S(2)}) collective-permute-start(bf16[1024,384]{0,1:T(8,128)(2,1)} %get-tuple-element.30), channel_id=1, source_target_pairs={{0,4},{4,0},{8,12},{12,8},{1,5},{5,1},{9,13},{13,9},{2,6},{6,2},{1... | collective-permute-start | bytes 2359304 | tf_op jit(solution)/shard_map/output_gradient_over_mp/ppermute | solution.py:125
  119.1 46.7 %collective-permute-start.42 = (bf16[384,1024]{1,0:T(8,128)(2,1)S(1)}, bf16[384,1024]{1,0:T(8,128)(2,1)}, u32[]{:S(2)}, u32[]{:S(2)}) collective-permute-start(bf16[384,1024]{1,0:T(8,128)(2,1)S(1)} %get-tuple-element.20), channel_id=1, source_target_pairs={{0,1},{4,5},{8,9},{12,13},{16,17},{20,21},{24,25},{28,29}} | collective-permute-start | bytes 2359304 | tf_op jit(solution)/shard_map/weight_gradient_along_dp/ppermute | solution.py:95
  127.0 42.1 %collective-permute-start.39 = (bf16[384,1024]{1,0:T(8,128)(2,1)S(1)}, bf16[384,1024]{1,0:T(8,128)(2,1)}, u32[]{:S(2)}, u32[]{:S(2)}) collective-permute-start(bf16[384,1024]{1,0:T(8,128)(2,1)S(1)} %get-tuple-element.17), channel_id=1, source_target_pairs={{3,2},{7,6},{11,10},{15,14},{19,18},{23,22},{27,26},{31,30}} | collective-permute-start | bytes 2359304 | tf_op jit(solution)/shard_map/weight_gradient_along_dp/ppermute | solution.py:95
  129.8 47.9 %collective-permute-start.25 = (bf16[384,1024]{1,0:T(8,128)(2,1)}, bf16[384,1024]{1,0:T(8,128)(2,1)}, u32[]{:S(2)}, u32[]{:S(2)}) collective-permute-start(bf16[384,1024]{1,0:T(8,128)(2,1)} %fusion.81), channel_id=1, source_target_pairs={{0,1},{1,2},{4,5},{5,6},{8,9},{9,10},{12,13},{13,14},{16,17},{17,1... | collective-permute-start | bytes 2359304 | tf_op jit(solution)/shard_map/weight_gradient_along_dp/ppermute | solution.py:95
  135.1 59.5 %collective-permute-start.31 = (bf16[384,1024]{1,0:T(8,128)(2,1)}, bf16[384,1024]{1,0:T(8,128)(2,1)}, u32[]{:S(2)}, u32[]{:S(2)}) collective-permute-start(bf16[384,1024]{1,0:T(8,128)(2,1)} %fusion.75), channel_id=1, source_target_pairs={{0,1},{1,2},{4,5},{5,6},{8,9},{9,10},{12,13},{13,14},{16,17},{17,1... | collective-permute-start | bytes 2359304 | tf_op jit(solution)/shard_map/weight_gradient_along_dp/ppermute | solution.py:95
  146.6 103.0 %collective-permute-start.12 = (bf16[512,1536]{1,0:T(8,128)(2,1)}, bf16[512,1536]{1,0:T(8,128)(2,1)}, u32[]{:S(2)}, u32[]{:S(2)}) collective-permute-start(bf16[512,1536]{1,0:T(8,128)(2,1)} %get-tuple-element.23), channel_id=1, source_target_pairs={{0,1},{1,2},{2,3},{4,5},{5,6},{6,7},{8,9},{9,10},{10,11},{12,13},{... | collective-permute-start | bytes 4718600 | tf_op jit(solution)/shard_map/projection_along_dp/ppermute | solution.py:95
  165.8 79.2 %collective-permute-start.37 = (bf16[384,1024]{1,0:T(8,128)(2,1)S(1)}, bf16[384,1024]{1,0:T(8,128)(2,1)S(1)}, u32[]{:S(2)}, u32[]{:S(2)}) collective-permute-start(bf16[384,1024]{1,0:T(8,128)(2,1)S(1)} %fusion.69), channel_id=1, source_target_pairs={{0,1},{1,2},{4,5},{5,6},{8,9},{9,10},{12,13},{13,14},{16,17},{17,1... | collective-permute-start | bytes 2359304 | tf_op jit(solution)/shard_map/weight_gradient_along_dp/ppermute | solution.py:95
  169.2 82.0 %collective-permute-start.45 = (bf16[384,1024]{1,0:T(8,128)(2,1)}, bf16[384,1024]{1,0:T(8,128)(2,1)}, u32[]{:S(2)}, u32[]{:S(2)}) collective-permute-start(bf16[384,1024]{1,0:T(8,128)(2,1)} %get-tuple-element.21), channel_id=1, source_target_pairs={{3,2},{7,6},{11,10},{15,14},{19,18},{23,22},{27,26},{31,30}} | collective-permute-start | bytes 2359304 | tf_op jit(solution)/shard_map/weight_gradient_along_dp/ppermute | solution.py:95
  177.7 89.3 %collective-permute-start.14 = (bf16[512,1536]{1,0:T(8,128)(2,1)}, bf16[512,1536]{1,0:T(8,128)(2,1)}, u32[]{:S(2)}, u32[]{:S(2)}) collective-permute-start(bf16[512,1536]{1,0:T(8,128)(2,1)} %collective-permute-done.13), channel_id=1, source_target_pairs={{1,0},{2,1},{5,4},{6,5},{9,8},{10,9},{13,12},{14,13},{17,16},{18,1... | collective-permute-start | bytes 4718600 | tf_op jit(solution)/shard_map/projection_along_dp/ppermute | solution.py:95
  194.6 66.7 %collective-permute-start.43 = (bf16[384,1024]{1,0:T(8,128)(2,1)S(1)}, bf16[384,1024]{1,0:T(8,128)(2,1)}, u32[]{:S(2)}, u32[]{:S(2)}) collective-permute-start(bf16[384,1024]{1,0:T(8,128)(2,1)S(1)} %fusion.63), channel_id=1, source_target_pairs={{0,1},{1,2},{4,5},{5,6},{8,9},{9,10},{12,13},{13,14},{16,17},{17,1... | collective-permute-start | bytes 2359304 | tf_op jit(solution)/shard_map/weight_gradient_along_dp/ppermute | solution.py:95
  267.0 46.5 %collective-permute-start.26 = (bf16[384,1024]{1,0:T(8,128)(2,1)S(1)}, bf16[384,1024]{1,0:T(8,128)(2,1)S(1)}, u32[]{:S(2)}, u32[]{:S(2)}) collective-permute-start(bf16[384,1024]{1,0:T(8,128)(2,1)S(1)} %copy-done.35), channel_id=1, source_target_pairs={{0,1},{1,2},{2,3},{4,5},{5,6},{6,7},{8,9},{9,10},{10,11},{12,13},{... | collective-permute-start | bytes 2359304 | tf_op jit(solution)/shard_map/weight_gradient_along_dp/ppermute | solution.py:95
  272.4 42.4 %collective-permute-start.32 = (bf16[384,1024]{1,0:T(8,128)(2,1)S(1)}, bf16[384,1024]{1,0:T(8,128)(2,1)S(1)}, u32[]{:S(2)}, u32[]{:S(2)}) collective-permute-start(bf16[384,1024]{1,0:T(8,128)(2,1)S(1)} %copy-done.34), channel_id=1, source_target_pairs={{0,1},{1,2},{2,3},{4,5},{5,6},{6,7},{8,9},{9,10},{10,11},{12,13},{... | collective-permute-start | bytes 2359304 | tf_op jit(solution)/shard_map/weight_gradient_along_dp/ppermute | solution.py:95
  274.4 49.6 %collective-permute-start.38 = (bf16[384,1024]{1,0:T(8,128)(2,1)}, bf16[384,1024]{1,0:T(8,128)(2,1)S(1)}, u32[]{:S(2)}, u32[]{:S(2)}) collective-permute-start(bf16[384,1024]{1,0:T(8,128)(2,1)} %get-tuple-element.14), channel_id=1, source_target_pairs={{0,1},{1,2},{2,3},{4,5},{5,6},{6,7},{8,9},{9,10},{10,11},{12,13},{... | collective-permute-start | bytes 2359304 | tf_op jit(solution)/shard_map/weight_gradient_along_dp/ppermute | solution.py:95
  298.9 53.1 %collective-permute-start.44 = (bf16[384,1024]{1,0:T(8,128)(2,1)}, bf16[384,1024]{1,0:T(8,128)(2,1)S(1)}, u32[]{:S(2)}, u32[]{:S(2)}) collective-permute-start(bf16[384,1024]{1,0:T(8,128)(2,1)} %get-tuple-element.18), channel_id=1, source_target_pairs={{0,1},{1,2},{2,3},{4,5},{5,6},{6,7},{8,9},{9,10},{10,11},{12,13},{... | collective-permute-start | bytes 2359304 | tf_op jit(solution)/shard_map/weight_gradient_along_dp/ppermute | solution.py:95
  313.5 107.9 %collective-permute-start.15 = (bf16[512,1536]{1,0:T(8,128)(2,1)}, bf16[512,1536]{1,0:T(8,128)(2,1)}, u32[]{:S(2)}, u32[]{:S(2)}) collective-permute-start(bf16[512,1536]{1,0:T(8,128)(2,1)} %collective-permute-done.14), channel_id=1, source_target_pairs={{1,0},{5,4},{9,8},{13,12},{17,16},{21,20},{25,24},{29,28}} | collective-permute-start | bytes 4718600 | tf_op jit(solution)/shard_map/projection_along_dp/ppermute | solution.py:95
  314.9 55.9 %collective-permute-start.29 = (bf16[384,1024]{1,0:T(8,128)(2,1)}, bf16[384,1024]{1,0:T(8,128)(2,1)}, u32[]{:S(2)}, u32[]{:S(2)}) collective-permute-start(bf16[384,1024]{1,0:T(8,128)(2,1)} %fusion.80), channel_id=1, source_target_pairs={{1,0},{2,1},{3,2},{5,4},{6,5},{7,6},{9,8},{10,9},{11,10},{13,12},{... | collective-permute-start | bytes 2359304 | tf_op jit(solution)/shard_map/weight_gradient_along_dp/ppermute | solution.py:95
  323.9 63.7 %collective-permute-start.35 = (bf16[384,1024]{1,0:T(8,128)(2,1)}, bf16[384,1024]{1,0:T(8,128)(2,1)}, u32[]{:S(2)}, u32[]{:S(2)}) collective-permute-start(bf16[384,1024]{1,0:T(8,128)(2,1)} %fusion.74), channel_id=1, source_target_pairs={{1,0},{2,1},{3,2},{5,4},{6,5},{7,6},{9,8},{10,9},{11,10},{13,12},{... | collective-permute-start | bytes 2359304 | tf_op jit(solution)/shard_map/weight_gradient_along_dp/ppermute | solution.py:95
  325.2 76.1 %collective-permute-start.41 = (bf16[384,1024]{1,0:T(8,128)(2,1)}, bf16[384,1024]{1,0:T(8,128)(2,1)}, u32[]{:S(2)}, u32[]{:S(2)}) collective-permute-start(bf16[384,1024]{1,0:T(8,128)(2,1)} %fusion.68), channel_id=1, source_target_pairs={{1,0},{2,1},{3,2},{5,4},{6,5},{7,6},{9,8},{10,9},{11,10},{13,12},{... | collective-permute-start | bytes 2359304 | tf_op jit(solution)/shard_map/weight_gradient_along_dp/ppermute | solution.py:95
  351.9 76.7 %collective-permute-start.19 = (bf16[512,1536]{1,0:T(8,128)(2,1)}, bf16[512,1536]{1,0:T(8,128)(2,1)S(1)}, u32[]{:S(2)}, u32[]{:S(2)}) collective-permute-start(bf16[512,1536]{1,0:T(8,128)(2,1)} %collective-permute-done.18), channel_id=1, source_target_pairs={{2,18},{3,19},{18,2},{19,3},{6,22},{7,23},{22,6},{23,7},{10,26},{1... | collective-permute-start | bytes 4718600 | tf_op jit(solution)/shard_map/attended_gradient/ppermute | solution.py:101
  370.7 60.1 %collective-permute-start.21 = (bf16[512,1536]{1,0:T(8,128)(2,1)}, bf16[512,1536]{1,0:T(8,128)(2,1)}, u32[]{:S(2)}, u32[]{:S(2)}) collective-permute-start(bf16[512,1536]{1,0:T(8,128)(2,1)} %collective-permute-done.18), channel_id=1, source_target_pairs={{2,3},{6,7},{10,11},{14,15},{18,19},{22,23},{26,27},{30,31}} | collective-permute-start | bytes 4718600 | tf_op jit(solution)/shard_map/projection_along_dp/ppermute | solution.py:95
  387.6 56.9 %collective-permute-start.20 = (bf16[512,1536]{1,0:T(8,128)(2,1)}, bf16[512,1536]{1,0:T(8,128)(2,1)}, u32[]{:S(2)}, u32[]{:S(2)}) collective-permute-start(bf16[512,1536]{1,0:T(8,128)(2,1)} %collective-permute-done.14), channel_id=1, source_target_pairs={{0,16},{1,17},{16,0},{17,1},{4,20},{5,21},{20,4},{21,5},{8,24},{9,... | collective-permute-start | bytes 4718600 | tf_op jit(solution)/shard_map/attended_gradient/ppermute | solution.py:101
  428.6 61.1 %collective-permute-start.23 = (bf16[512,1536]{1,0:T(8,128)(2,1)}, bf16[512,1536]{1,0:T(8,128)(2,1)S(1)}, u32[]{:S(2)}, u32[]{:S(2)}) collective-permute-start(bf16[512,1536]{1,0:T(8,128)(2,1)} %collective-permute-done.13), channel_id=1, source_target_pairs={{0,16},{1,17},{2,18},{16,0},{17,1},{18,2},{4,20},{5,21},{6,22},{20... | collective-permute-start | bytes 4718600 | tf_op jit(solution)/shard_map/attended_gradient/ppermute | solution.py:101
  430.8 58.9 %collective-permute-start.22 = (bf16[512,1536]{1,0:T(8,128)(2,1)}, bf16[512,1536]{1,0:T(8,128)(2,1)}, u32[]{:S(2)}, u32[]{:S(2)}) collective-permute-start(bf16[512,1536]{1,0:T(8,128)(2,1)} %collective-permute-done.21), channel_id=1, source_target_pairs={{3,19},{19,3},{7,23},{23,7},{11,27},{27,11},{15,31},{31,15}} | collective-permute-start | bytes 4718600 | tf_op jit(solution)/shard_map/attended_gradient/ppermute | solution.py:101
  (71 other events, 1948.3 us)

commit v2 on v0

v2 whole, which is shorter than its diff:
```python
import functools
import math

import jax
import jax.numpy as jnp
from jax import lax
from jax.experimental import pallas as pl
from jax.experimental.pallas import tpu as pltpu
from jax.sharding import PartitionSpec as P

HD = 128
LEN = 512
SCALE = 1.0 / math.sqrt(HD)
CHUNKS = 3
LIGHT = 20
NT = (((1,), (1,)), ((), ()))
NN = (((1,), (0,)), ((), ()))
TN = (((0,), (0,)), ((), ()))
ROOM = pltpu.CompilerParams(vmem_limit_bytes=48 * 2**20)


def dot(a, b, dims):
    return lax.dot_general(a, b, dims, preferred_element_type=jnp.float32)


def cost(flops, moved):
    return pl.CostEstimate(flops=flops // LIGHT, bytes_accessed=moved // LIGHT, transcendentals=0)


def after(array, *others):
    return lax.optimization_barrier((array, *others))[0]


def probabilities(queries, keys, allowed):
    scores = jnp.where(allowed, dot(queries, keys, NT) * SCALE, -jnp.inf)
    exponent = jnp.exp(scores - jnp.max(scores, axis=-1, keepdims=True))
    return exponent * (1.0 / jnp.sum(exponent, axis=-1, keepdims=True))


def forward_kernel(column_ids, row_ids, qkv, attended):
    allowed = column_ids[0] == row_ids[0]
    for head in range(attended.shape[0] // HD):
        cols = slice(head * HD, (head + 1) * HD)
        weights = probabilities(qkv[0, :, cols], qkv[1, :, cols], allowed).astype(jnp.bfloat16)
        attended[cols, :] = dot(weights, qkv[2, :, cols], NN).astype(jnp.bfloat16).T


def backward_kernel(column_ids, row_ids, qkv, grad_att, *refs):
    grad_qkv = refs[-1]
    allowed = column_ids[0] == row_ids[0]
    for head in range(grad_att.shape[1] // HD):
        cols = slice(head * HD, (head + 1) * HD)
        queries, keys, values = qkv[0, :, cols], qkv[1, :, cols], qkv[2, :, cols]
        grads = grad_att[:, cols]
        probability = probabilities(queries, keys, allowed)
        grad_probs = dot(grads, values, NT)
        row_dot = jnp.sum(probability * grad_probs, axis=-1, keepdims=True)
        grad_scores = (probability * (grad_probs - row_dot) * SCALE).astype(jnp.bfloat16)
        weights = probability.astype(jnp.bfloat16)
        grad_qkv[0, :, cols] = dot(grad_scores, keys, NN).astype(jnp.bfloat16)
        grad_qkv[1, :, cols] = dot(grad_scores, queries, TN).astype(jnp.bfloat16)
        grad_qkv[2, :, cols] = dot(weights, grads, TN).astype(jnp.bfloat16)


def attention_specs(segments, qkv, start):
    seqs = qkv.shape[1] // LEN
    block = 2 * HD
    three = pl.BlockSpec((3, LEN, block), lambda s, h: (0, start + s, h))
    in_specs = [
        pl.BlockSpec((1, LEN, 1), lambda s, h: (start + s, 0, 0)),
        pl.BlockSpec((1, 1, LEN), lambda s, h: (start + s, 0, 0)),
        three,
    ]
    return in_specs, [segments.reshape(seqs, LEN, 1), segments.reshape(seqs, 1, LEN), qkv]


def attention_forward(segments, qkv):
    tokens, width = qkv.shape[1:]
    block = 2 * HD
    in_specs, operands = attention_specs(segments, qkv, 0)
    return pl.pallas_call(
        forward_kernel,
        grid=(tokens // LEN, width // block),
        in_specs=in_specs,
        out_specs=pl.BlockSpec((block, LEN), lambda s, h: (h, s)),
        out_shape=jax.ShapeDtypeStruct((width, tokens), jnp.bfloat16),
        compiler_params=ROOM,
        cost_estimate=cost(2 * 2 * tokens * LEN * width, 8 * tokens * width),
    )(*operands)


def attention_backward(segments, qkv, grad_att, start, into):
    tokens, width = qkv.shape[1:]
    block = 2 * HD
    rows = grad_att.shape[0]
    in_specs, operands = attention_specs(segments, qkv, start)
    in_specs.append(pl.BlockSpec((LEN, block), lambda s, h: (s, h)))
    operands.append(grad_att)
    if into is not None:
        in_specs.append(pl.BlockSpec(memory_space=pl.ANY))
        operands.append(into)
    return pl.pallas_call(
        backward_kernel,
        grid=(rows // LEN, width // block),
        in_specs=in_specs,
        out_specs=in_specs[2],
        out_shape=jax.ShapeDtypeStruct(qkv.shape, jnp.bfloat16),
        input_output_aliases={} if into is None else {4: 0},
        compiler_params=ROOM,
        cost_estimate=cost(2 * 5 * rows * LEN * width, 14 * rows * width),
    )(*operands)


def partial_kernel(order, attended, *refs):
    *features, pair, third, own, held = refs
    for at, block in enumerate(features):
        held[at] = dot(attended[...], block[...], NN)
    for at, out in enumerate((pair.at[0], pair.at[1], third, own)):
        out[...] = held[order[at]].astype(out.dtype)


def partial_call(order, attended, features):
    width, tokens = attended.shape
    chunk = features[0].shape[1]
    rows = min(256, width)
    out = pl.BlockSpec((rows, chunk), lambda r, _: (r, 0))
    return pl.pallas_call(
        partial_kernel,
        grid_spec=pltpu.PrefetchScalarGridSpec(
            num_scalar_prefetch=1,
            grid=(width // rows,),
            in_specs=[pl.BlockSpec((rows, tokens), lambda r, _: (r, 0))]
            + [pl.BlockSpec((tokens, chunk), lambda r, _: (0, 0)) for _ in features],
            out_specs=[pl.BlockSpec((2, rows, chunk), lambda r, _: (0, r, 0)), out, out],
            scratch_shapes=[pltpu.VMEM((len(features), rows, chunk), jnp.float32)],
        ),
        out_shape=[
            jax.ShapeDtypeStruct((2, width, chunk), jnp.bfloat16),
            jax.ShapeDtypeStruct((width, chunk), jnp.bfloat16),
            jax.ShapeDtypeStruct((width, chunk), jnp.float32),
        ],
        compiler_params=ROOM,
        cost_estimate=cost(
            2 * len(features) * chunk * width * tokens,
            2 * len(features) * chunk * (tokens + width) + 2 * width * tokens,
        ),
    )(order, attended, *features)


def attended_kernel(order, *refs):
    *features, own, one, one_far, two, two_far, three, three_far, out, held = refs
    blocks = held.shape[0]
    pieces = len(features) // blocks
    half = one.shape[0]
    for at in range(blocks):
        start = 0
        for piece in features[at * pieces : (at + 1) * pieces]:
            stop = start + piece.shape[1]
            held[at, :, start:stop] = piece[...]
            start = stop
    near_start = pl.multiple_of(order[4] * half, HD)
    far_start = pl.multiple_of((1 - order[4]) * half, HD)
    near = dot(held[order[0]], own[pl.ds(near_start, half), :], NT)
    far = dot(held[order[0]], own[pl.ds(far_start, half), :], NT)
    for slot, (here, there) in enumerate(((one, one_far), (two, two_far), (three, three_far))):
        near += dot(held[order[slot + 1]], here[...], NT)
        far += dot(held[order[slot + 1]], there[...], NT)
    out[:, pl.ds(near_start, half)] = near.astype(jnp.bfloat16)
    out[:, pl.ds(far_start, half)] = far.astype(jnp.bfloat16)


def attended_call(order, gathered, weights, start, tokens):
    width, own_width = weights[0].shape
    blocks = len(gathered[0])
    features = [pieces[at] for at in range(blocks) for pieces in gathered]
    rows = min(256, tokens)
    skip = start // rows
    return pl.pallas_call(
        attended_kernel,
        grid_spec=pltpu.PrefetchScalarGridSpec(
            num_scalar_prefetch=1,
            grid=(tokens // rows,),
            in_specs=[pl.BlockSpec((rows, f.shape[1]), lambda r, _: (skip + r, 0)) for f in features]
            + [
                pl.BlockSpec(w.shape, lambda r, _: (0, 0), pipeline_mode=pl.Buffered(1))
                for w in weights
            ],
            out_specs=pl.BlockSpec((rows, width), lambda r, _: (r, 0)),
            scratch_shapes=[pltpu.VMEM((blocks, rows, own_width), jnp.bfloat16)],
        ),
        out_shape=jax.ShapeDtypeStruct((tokens, width), jnp.bfloat16),
        compiler_params=ROOM,
        cost_estimate=cost(
            2 * tokens * width * blocks * own_width,
            2 * (blocks * own_width * (tokens + width) + tokens * width),
        ),
    )(order, *features, *weights)


def plain_shards(qkv, grad_out, out_weight, segments):
    attended = attention_forward(segments, qkv)
    rows = lax.all_gather(grad_out.astype(jnp.bfloat16), "mp", axis=1, tiled=True)
    projection = lax.all_gather(out_weight, "dp", axis=1, tiled=True)
    block = dot(attended, rows, NN)
    grad_weight = lax.psum_scatter(block, "dp", scatter_dimension=1, tiled=True)
    grad_att = dot(rows, projection, NT).astype(jnp.bfloat16)
    grad_qkv = attention_backward(segments, qkv, grad_att, 0, None)
    return grad_qkv, grad_weight.astype(jnp.bfloat16)


OUTER = [(0, 1), (1, 0), (2, 3), (3, 2)]
INWARD = [(0, 1), (3, 2)]
MIDDLE = [(1, 2), (2, 1)]
OUTWARD = [(1, 0), (2, 3)]


def shards(qkv, grad_out, out_weight, segments):
    width = qkv.shape[2]
    own_width = grad_out.shape[1]
    chunk = own_width // CHUNKS
    group = lax.axis_index("groups")
    here = lax.axis_index("mp")
    place = lax.axis_index("dp")
    outer = (place == 0) | (place == 3)
    low = place < 2

    def along(array, pairs):
        return lax.ppermute(array, "dp", pairs)

    def swap_groups(array):
        return lax.ppermute(array, "groups", [(0, 1), (1, 0)])

    last = []

    def chained(array, *others):
        return after(array, *last, *others)

    def done(*arrays):
        last[:] = arrays[:1]
        return arrays[0] if len(arrays) == 1 else arrays

    half = width // 2
    own_half = lax.dynamic_slice_in_dim(out_weight, group * half, half, 0)
    first = along(own_half, OUTER)
    middle = along(own_half, MIDDLE)
    first_far = swap_groups(first)
    middle_second = along(first, MIDDLE)
    outward = along(middle, OUTWARD)
    outward_second = along(middle_second, OUTWARD)

    attended = done(attention_forward(segments, qkv))

    partial_order = jnp.stack(
        [
            jnp.where(low, 3, 0) ^ here,
            jnp.where(low, 2, 1) ^ here,
            jnp.where(outer, jnp.where(low, 1, 2), jnp.where(low, 0, 3)) ^ here,
            place ^ here,
        ]
    ).astype(jnp.int32)
    gathered, partials = [], []

    def gather(c):
        mine = grad_out[:, c * chunk : (c + 1) * chunk].astype(jnp.bfloat16)
        if c:
            mine = after(mine, attended)
        near = lax.ppermute(mine, "mp", [(i, i ^ 1) for i in range(4)])
        across = lax.ppermute(mine, "mp", [(i, i ^ 2) for i in range(4)])
        both = lax.ppermute(chained(across), "mp", [(i, i ^ 1) for i in range(4)])
        gathered.append([mine, near, across, both])

    def partial(c, *others):
        partials.append(
            done(*partial_call(chained(partial_order, *others), attended, gathered[c]))
        )

    pairs_in, last_in, middle_sums, outward_sums = [], [], [], []

    def send_pair(c, *others):
        value = partials[c][0]
        if others:
            value = after(value, *others)
        pairs_in.append(along(value, INWARD))

    def send_last(c, *others):
        last_in.append(along(after(partials[c][1], *others), INWARD))

    def send_middle(t, c, *others):
        mine, arrived = chained(partials[c][0], *others)[t], pairs_in[c][t]
        value = mine.astype(jnp.float32) + arrived.astype(jnp.float32)
        middle_sums.append(along(done(value.astype(jnp.bfloat16)), MIDDLE))

    def send_outward(c, *others):
        arrived = middle_sums[2 * c]
        value = chained(partials[c][1], *others).astype(jnp.float32)
        value = value + arrived.astype(jnp.float32)
        outward_sums.append(along(done(value.astype(jnp.bfloat16)), OUTWARD))

    grads = [None]
    attended_order = jnp.stack(
        [
            place ^ here,
            (place ^ 1) ^ here,
            jnp.where(low, 2, 1) ^ here,
            jnp.where(low, 3, 0) ^ here,
            group,
        ]
    ).astype(jnp.int32)
    grad_att = []

    def attended_gradient(s, *others):
        weights = [out_weight, first, first_far, second, second_far, third, third_far]
        found = attended_call(chained(attended_order, *others), gathered, weights, s * LEN, LEN)
        grad_att.append(done(found))

    def backward(s, *others):
        grads.append(
            done(attention_backward(segments, qkv, chained(grad_att[s], *others), s, grads[-1]))
        )

    def finish(c, into):
        total = chained(partials[c][2])
        for part in (middle_sums[2 * c + 1], outward_sums[c], last_in[c]):
            total = total + part.astype(jnp.float32)
        return done(
            lax.dynamic_update_slice_in_dim(into, total.astype(jnp.bfloat16), c * chunk, 1)
        )

    gather(0)
    partial(0)
    send_pair(0, first, middle)
    gather(1)
    partial(1, middle_second)
    gather(2)
    send_pair(1)
    send_middle(0, 0)
    second = done(chained(middle, outward) + outward)
    second_far = swap_groups(second)
    send_middle(1, 0)
    partial(2, first_far)
    send_pair(2, pairs_in[0])
    send_outward(0)
    third = done(chained(middle_second, outward_second) + outward_second)
    third_far = swap_groups(third)
    send_middle(0, 1, second_far)
    send_last(0, pairs_in[1])
    send_middle(1, 1, middle_sums[1])
    attended_gradient(0)
    send_outward(1, outward_sums[0])
    send_middle(0, 2)
    attended_gradient(1)
    send_last(1, pairs_in[1])
    send_middle(1, 2, outward_sums[1], last_in[0])
    backward(0, middle_sums[3])
    send_outward(2)
    grad_weight = jnp.zeros((width, own_width), jnp.bfloat16)
    grad_weight = finish(0, grad_weight)
    send_last(2, pairs_in[2])
    backward(1, last_in[1])
    grad_weight = finish(1, grad_weight)
    grad_weight = finish(2, grad_weight)
    return grads[-1], grad_weight


def solution(mesh):
    line = [mesh.shape[name] for name in ("groups", "mp", "dp")] == [2, 4, 4]
    return jax.shard_map(
        shards if line else plain_shards,
        mesh=mesh,
        in_specs=(
            P(None, ("groups", "dp"), "mp"),
            P(("groups", "dp"), "mp"),
            P("mp", "dp"),
            P(("groups", "dp"), None),
        ),
        out_specs=(P(None, ("groups", "dp"), "mp"), P(("groups", "mp"), "dp")),
        check_vma=False,
    )
```

time: 745 us -> 279 us (0.37)
  waiting for transfers between devices: 517 us -> 57.4 us
  matrix products: 111 us -> 0 us
  Pallas kernels: 0 us -> 90.2 us
  starting transfers between devices: 0.12 us -> 87.7 us
  local copies, waits for them, and re-layouts: 59.4 us -> 9.69 us
  between operations: 13.8 us -> 1.1 us
  other arithmetic: 41.5 us -> 31.4 us
    reduce_scatter x1 -> x0, waiting for transfers between devices: 294 us -> none  [shards(): lax.psum_scatter(block, 'dp', scatter_dimension=1, tiled=True)]
    all_gather x2 -> x0, waiting for transfers between devices: 222 us -> none  [the longest x1 198 us: shards(): projection = lax.all_gather(out_weight, 'dp', axis=1, tiled=True)]
    dot_general x14 -> x0, matrix products: 93.3 us -> none  [the longest x1 21.5 us: shards(): lax.dot_general(attended_rows, piece, (((0,), (0,)), ((), ())), preferred...]
    pallas_call x0 -> x8, Pallas kernels: none -> 90.2 us  [the longest x2 26.9 us: attended_call(): pl.pallas_call(attended_kernel, grid_spec=pltpu.PrefetchScalarGridSpec(nu...]
    ppermute x0 -> x32, starting transfers between devices: none -> 87.7 us  [the longest x20 77 us: along(): return lax.ppermute(array, 'dp', pairs)]
    ppermute x0 -> x32, waiting for transfers between devices: none -> 57.4 us  [the longest x20 39.3 us: along(): return lax.ppermute(array, 'dp', pairs)]
    dynamic_slice x16 -> x1, local copies, waits for them, and re-layouts: 24.3 us -> 2.72 us  [shards(): own_half = lax.dynamic_slice_in_dim(out_weight, group * half, half, 0)]
    sub x2 -> x0, matrix products: 17.9 us -> none  [backward(): grad_probs - row_dot]
  transfers between devices with their start and end apart: 3 -> 32, of which waited for: 3 -> 7; matrix products, arithmetic and copies ran while one was open for 27% -> 11% of each run, Pallas kernels for 0% -> 33%
where the time goes in v2:
time: 279 us; the launch traced here: 277 us
  Pallas kernels  90.2 us (32%)
  starting transfers between devices  87.7 us (31%)
  waiting for transfers between devices  57.4 us (21%)
  other arithmetic  31.4 us (11%)
  local copies, waits for them, and re-layouts  9.69 us (3%)
    ppermute x20, starting transfers between devices, along(): return lax.ppermute(array, 'dp', pairs)  77 us
    ppermute x20, waiting for transfers between devices, along(): return lax.ppermute(array, 'dp', pairs)  39.3 us
    pallas_call x2, Pallas kernels, attended_call(): pl.pallas_call(attended_kernel, grid_spec=pltpu.PrefetchScalarGridSpec(nu...  26.9 us
    pallas_call x3, Pallas kernels, partial_call(): pl.pallas_call(partial_kernel, grid_spec=pltpu.PrefetchScalarGridSpec(num...  25.8 us
    pallas_call x2, Pallas kernels, attention_backward(): pl.pallas_call(backward_kernel, grid=(rows // LEN, width // block), in_sp...  24.4 us
    ppermute x3, waiting for transfers between devices, gather(): across = lax.ppermute(mine, 'mp', [(i, i ^ 2) for i in range(4)])  16.1 us
    pallas_call x1, Pallas kernels, attention_forward(): pl.pallas_call(forward_kernel, grid=(tokens // LEN, width // block), in_s...  13 us
    convert_element_type x6, other arithmetic, send_middle(): middle_sums.append(along(done(value.astype(jnp.bfloat16)), MIDDLE))  10.9 us
  transfers between devices with their start and end apart: 32, of which 7 were waited for; matrix products, arithmetic and copies ran while one was open for 11% of the time, Pallas kernels for 33%

profile of v2, /device:TPU:0, one launch (start us, length us, event | category | flops | bytes accessed | tf_op | source)
XLA Modules:
  0.0 277.4 jit_solution(7046334624491583397)
XLA Ops:
  0.6 3.2 %convert.5 = bf16[1024,1536]{1,0:T(8,128)(2,1)S(1)} convert(f32[1024,1536]{1,0:T(8,128)} %param.5) | non-fusion elementwise | flops 1572864 | bytes 9437184 | tf_op jit(solution)/shard_map/convert.2
  4.1 3.0 %collective-permute-start.1 = (bf16[1024,512]{1,0:T(8,128)(2,1)S(1)}, bf16[1024,512]{1,0:T(8,128)(2,1)}, u32[]{:S(2)}, u32[]{:S(2)}) collective-permute-start(bf16[1024,512]{1,0:T(8,128)(2,1)S(1)} %get-tuple-element.84.refs_0_), channel_id=1, source_target_pairs={{0,8},{4,12},{8,0},{12,4},{1,9},{5,13},{9,1},{13,5},{2,10},{6,14},... | collective-permute-start | bytes 3145736 | tf_op jit(solution)/shard_map/ppermute | solution.py:268
  7.1 2.7 constant_dynamic-slice_fusion
  15.4 13.0 %shard_map.59.attended = bf16[1024,1024]{1,0:T(8,128)(2,1)S(1)} custom-call(s32[2,512,1]{2,1,0:T(8,128)S(1)} %copy-done.6, s32[2,1,512]{2,1,0:T(1,128)S(1)} %reshape.39.row_ids, bf16[3,1024,1024]{2,1,0:T(8,128)(2,1)} %qkv.5), custom_call_target="tpu_custom_call" | custom-call | flops 107374184 | bytes 419430 | tf_op jit(solution)/shard_map/pallas_call | solution.py:81
  32.1 13.9 %collective-permute-done.4.refs_13_ = bf16[512,1536]{1,0:T(8,128)(2,1)} collective-permute-done((bf16[512,1536]{1,0:T(8,128)(2,1)}, bf16[512,1536]{1,0:T(8,128)(2,1)}, u32[]{:S(2)}, u32[]{:S(2)}) %collective-permute-start.4) | collective-permute-done | bytes 1572896 | tf_op jit(solution)/shard_map/ppermute | solution.py:228
  47.9 9.1 %shard_map.60 = (bf16[2,1024,512]{2,1,0:T(8,128)(2,1)}, bf16[1024,512]{1,0:T(8,128)(2,1)S(1)}, f32[1024,512]{1,0:T(8,128)}) custom-call(s32[4]{0:T(128)S(1)} %pad_add_fusion.order, bf16[1024,1024]{1,0:T(8,128)(2,1)} %copy-done, bf16[1024,512]{1,0:T(8,128)(2,1)S(1)} %get-tuple-element.84.refs_0_, bf16[1024,512]{1,0:T(8,128)(2,1)} %collective-permute-done.refs_1_.refs_3_, ...), custom_call_target="tpu_custom_call" | custom-call | flops 214748368 | bytes 524288 | tf_op jit(solution)/shard_map/pallas_call | solution.py:127
  57.6 6.5 %collective-permute-start.9 = (bf16[2,1024,512]{2,1,0:T(8,128)(2,1)}, bf16[2,1024,512]{2,1,0:T(8,128)(2,1)}, u32[]{:S(2)}, u32[]{:S(2)}) collective-permute-start(bf16[2,1024,512]{2,1,0:T(8,128)(2,1)} %get-tuple-element.52), channel_id=1, source_target_pairs={{0,1},{3,2},{4,5},{7,6},{8,9},{11,10},{12,13},{15,14},{16,17},{19,... | collective-permute-start | bytes 6291464 | tf_op jit(solution)/shard_map/ppermute | solution.py:228
  67.6 8.5 %shard_map.61 = (bf16[2,1024,512]{2,1,0:T(8,128)(2,1)}, bf16[1024,512]{1,0:T(8,128)(2,1)S(1)}, f32[1024,512]{1,0:T(8,128)}) custom-call(s32[4]{0:T(128)S(1)} %pad_add_fusion.order, bf16[1024,1024]{1,0:T(8,128)(2,1)} %copy-done, bf16[1024,512]{1,0:T(8,128)(2,1)S(1)} %get-tuple-element.46.refs_0_.refs_1_, ...), custom_call_target="tpu_custom_call" | custom-call | flops 214748368 | bytes 524288 | tf_op jit(solution)/shard_map/pallas_call | solution.py:127
  76.1 15.5 %collective-permute-done.13.refs_2_.refs_8_ = bf16[1024,512]{1,0:T(8,128)(2,1)S(1)} collective-permute-done((bf16[1024,512]{1,0:T(8,128)(2,1)S(1)}, bf16[1024,512]{1,0:T(8,128)(2,1)S(1)}, u32[]{:S(2)}, u32[]{:S(2)}) %collective-permute-start.13) | collective-permute-done | bytes 1048608 | tf_op jit(solution)/shard_map/ppermute | solution.py:268
  91.5 5.5 %collective-permute-start.18 = (bf16[2,1024,512]{2,1,0:T(8,128)(2,1)}, bf16[2,1024,512]{2,1,0:T(8,128)(2,1)S(1)}, u32[]{:S(2)}, u32[]{:S(2)}) collective-permute-start(bf16[2,1024,512]{2,1,0:T(8,128)(2,1)} %get-tuple-element.62), channel_id=1, source_target_pairs={{0,1},{3,2},{4,5},{7,6},{8,9},{11,10},{12,13},{15,14},{16,17},{19,... | collective-permute-start | bytes 6291464 | tf_op jit(solution)/shard_map/ppermute | solution.py:228
  97.1 11.9 %collective-permute-done.9 = bf16[2,1024,512]{2,1,0:T(8,128)(2,1)} collective-permute-done((bf16[2,1024,512]{2,1,0:T(8,128)(2,1)}, bf16[2,1024,512]{2,1,0:T(8,128)(2,1)}, u32[]{:S(2)}, u32[]{:S(2)}) %collective-permute-start.9) | collective-permute-done | bytes 2097184 | tf_op jit(solution)/shard_map/ppermute | solution.py:228
  120.4 8.1 %shard_map.62 = (bf16[2,1024,512]{2,1,0:T(8,128)(2,1)}, bf16[1024,512]{1,0:T(8,128)(2,1)S(1)}, f32[1024,512]{1,0:T(8,128)}) custom-call(s32[4]{0:T(128)S(1)} %pad_add_fusion.order, bf16[1024,1024]{1,0:T(8,128)(2,1)} %copy-done, bf16[1024,512]{1,0:T(8,128)(2,1)S(1)} %get-tuple-element.54.refs_0_.refs_2_, ...), custom_call_target="tpu_custom_call" | custom-call | flops 214748368 | bytes 524288 | tf_op jit(solution)/shard_map/pallas_call | solution.py:127
  128.6 7.8 %collective-permute-start.23 = (bf16[2,1024,512]{2,1,0:T(8,128)(2,1)}, bf16[2,1024,512]{2,1,0:T(8,128)(2,1)}, u32[]{:S(2)}, u32[]{:S(2)}) collective-permute-start(bf16[2,1024,512]{2,1,0:T(8,128)(2,1)} %get-tuple-element.71), channel_id=1, source_target_pairs={{0,1},{3,2},{4,5},{7,6},{8,9},{11,10},{12,13},{15,14},{16,17},{19,... | collective-permute-start | bytes 6291464 | tf_op jit(solution)/shard_map/ppermute | solution.py:228
  136.4 2.6 add_convert_fusion.9
  139.0 7.0 %collective-permute-done.16 = bf16[512,1536]{1,0:T(8,128)(2,1)} collective-permute-done((bf16[512,1536]{1,0:T(8,128)(2,1)}, bf16[512,1536]{1,0:T(8,128)(2,1)}, u32[]{:S(2)}, u32[]{:S(2)}) %collective-permute-start.16) | collective-permute-done | bytes 1572896 | tf_op jit(solution)/shard_map/ppermute | solution.py:228
  145.9 3.4 %add.76.refs_17_ = bf16[512,1536]{1,0:T(8,128)(2,1)} add(bf16[512,1536]{1,0:T(8,128)(2,1)} %collective-permute-done.5, bf16[512,1536]{1,0:T(8,128)(2,1)} %collective-permute-done.16) | non-fusion elementwise | flops 786432 | bytes 4718592 | tf_op jit(solution)/shard_map/add | solution.py:343
  158.3 22.5 %collective-permute-start.25 = (bf16[1024,512]{1,0:T(8,128)(2,1)}, bf16[1024,512]{1,0:T(8,128)(2,1)S(1)}, u32[]{:S(2)}, u32[]{:S(2)}) collective-permute-start(bf16[1024,512]{1,0:T(8,128)(2,1)} %copy-done.8), channel_id=1, source_target_pairs={{0,1},{3,2},{4,5},{7,6},{8,9},{11,10},{12,13},{15,14},{16,17},{19,... | collective-permute-start | bytes 3145736 | tf_op jit(solution)/shard_map/ppermute | solution.py:228
  184.7 13.5 %shard_map.63.grad_att = bf16[512,1024]{1,0:T(8,128)(2,1)S(1)} custom-call(s32[5]{0:T(128)S(1)} %stack.32.order, bf16[1024,512]{1,0:T(8,128)(2,1)S(1)} %get-tuple-element.84.refs_0_, bf16[1024,512]{1,0:T(8,128)(2,1)S(1)} %get-tuple-element.46.refs_0_.refs_1_, bf16[1024,512]{1,0:T(8,128)(2,1)S(1)} %get-tuple-element.54.refs_0_.refs_2_, ...), custom_call_target="tpu_custom_call" | custom-call | flops 322122560 | bytes 996147 | tf_op jit(solution)/shard_map/pallas_call | solution.py:178
  205.2 11.4 %collective-permute-start.28 = (bf16[1024,512]{1,0:T(8,128)(2,1)S(1)}, bf16[1024,512]{1,0:T(8,128)(2,1)}, u32[]{:S(2)}, u32[]{:S(2)}) collective-permute-start(bf16[1024,512]{1,0:T(8,128)(2,1)S(1)} %copy-done.10), channel_id=1, source_target_pairs={{0,1},{3,2},{4,5},{7,6},{8,9},{11,10},{12,13},{15,14},{16,17},{19,... | collective-permute-start | bytes 3145736 | tf_op jit(solution)/shard_map/ppermute | solution.py:228
  216.6 13.5 %shard_map.64.grad_att = bf16[512,1024]{1,0:T(8,128)(2,1)S(1)} custom-call(s32[5]{0:T(128)S(1)} %stack.32.order, bf16[1024,512]{1,0:T(8,128)(2,1)S(1)} %get-tuple-element.84.refs_0_, bf16[1024,512]{1,0:T(8,128)(2,1)S(1)} %get-tuple-element.46.refs_0_.refs_1_, bf16[1024,512]{1,0:T(8,128)(2,1)S(1)} %get-tuple-element.54.refs_0_.refs_2_, ...), custom_call_target="tpu_custom_call" | custom-call | flops 322122560 | bytes 996147 | tf_op jit(solution)/shard_map/pallas_call | solution.py:178
  234.1 12.1 %shard_map.65.refs_0_ = bf16[3,1024,1024]{2,1,0:T(8,128)(2,1)} custom-call(s32[2,512,1]{2,1,0:T(8,128)S(1)} %copy-done.7, s32[2,1,512]{2,1,0:T(1,128)S(1)} %reshape.39.row_ids, bf16[3,1024,1024]{2,1,0:T(8,128)(2,1)} %qkv.5, bf16[512,1024]{1,0:T(8,128)(2,1)S(1)} %shard_map.63.grad_att), custom_call_target="tpu_custom_call" | custom-call | flops 134217728 | bytes 367001 | tf_op jit(solution)/shard_map/pallas_call | solution.py:102
  252.1 12.3 %shard_map.66 = bf16[3,1024,1024]{2,1,0:T(8,128)(2,1)} custom-call(s32[2,512,1]{2,1,0:T(8,128)S(1)} %copy-done.7, s32[2,1,512]{2,1,0:T(1,128)S(1)} %reshape.39.row_ids, bf16[3,1024,1024]{2,1,0:T(8,128)(2,1)} %qkv.5, bf16[512,1024]{1,0:T(8,128)(2,1)S(1)} %shard_map.64.grad_att, bf16[3,1024,1024]{2,1,0:T(8,128)(2,1)} %shard_map.65.refs_0_), custom_call_target="tpu_custom_call", output_to_operand_aliasing={{}: (4, {})} | custom-call | flops 134217728 | bytes 367001 | tf_op jit(solution)/shard_map/pallas_call | solution.py:102
  264.4 2.7 fusion.6
  267.1 6.5 %collective-permute-done.30 = bf16[1024,512]{1,0:T(8,128)(2,1)S(1)} collective-permute-done((bf16[1024,512]{1,0:T(8,128)(2,1)S(1)}, bf16[1024,512]{1,0:T(8,128)(2,1)S(1)}, u32[]{:S(2)}, u32[]{:S(2)}) %collective-permute-start.30) | collective-permute-done | bytes 1048608 | tf_op jit(solution)/shard_map/ppermute | solution.py:228
  (120 shorter events, 60.2 us)
Async XLA Ops:
  4.1 26.3 %collective-permute-start.1 = (bf16[1024,512]{1,0:T(8,128)(2,1)S(1)}, bf16[1024,512]{1,0:T(8,128)(2,1)}, u32[]{:S(2)}, u32[]{:S(2)}) collective-permute-start(bf16[1024,512]{1,0:T(8,128)(2,1)S(1)} %get-tuple-element.84.refs_0_), channel_id=1, source_target_pairs={{0,8},{4,12},{8,0},{12,4},{1,9},{5,13},{9,1},{13,5},{2,10},{6,14},... | collective-permute-start | bytes 3145736 | tf_op jit(solution)/shard_map/ppermute | solution.py:268
  9.8 36.2 %collective-permute-start.4 = (bf16[512,1536]{1,0:T(8,128)(2,1)}, bf16[512,1536]{1,0:T(8,128)(2,1)}, u32[]{:S(2)}, u32[]{:S(2)}) collective-permute-start(bf16[512,1536]{1,0:T(8,128)(2,1)} %constant_dynamic-slice_fusion), channel_id=1, source_target_pairs={{0,1},{1,0},{2,3},{3,2},{4,5},{5,4},{6,7},{7,6},{8,9},{9,8},{10,11... | collective-permute-start | bytes 4718600 | tf_op jit(solution)/shard_map/ppermute | solution.py:228
  11.4 46.2 %collective-permute-start.3 = (bf16[512,1536]{1,0:T(8,128)(2,1)}, bf16[512,1536]{1,0:T(8,128)(2,1)}, u32[]{:S(2)}, u32[]{:S(2)}) collective-permute-start(bf16[512,1536]{1,0:T(8,128)(2,1)} %constant_dynamic-slice_fusion), channel_id=1, source_target_pairs={{1,2},{2,1},{5,6},{6,5},{9,10},{10,9},{13,14},{14,13},{17,18},{18,... | collective-permute-start | bytes 4718600 | tf_op jit(solution)/shard_map/ppermute | solution.py:228
  13.3 34.6 %collective-permute-start = (bf16[1024,512]{1,0:T(8,128)(2,1)S(1)}, bf16[1024,512]{1,0:T(8,128)(2,1)}, u32[]{:S(2)}, u32[]{:S(2)}) collective-permute-start(bf16[1024,512]{1,0:T(8,128)(2,1)S(1)} %get-tuple-element.84.refs_0_), channel_id=1, source_target_pairs={{0,4},{4,0},{8,12},{12,8},{1,5},{5,1},{9,13},{13,9},{2,6},{6,2},{1... | collective-permute-start | bytes 3145736 | tf_op jit(solution)/shard_map/ppermute | solution.py:267
  30.3 26.7 %collective-permute-start.7 = (bf16[1024,512]{1,0:T(8,128)(2,1)S(1)}, bf16[1024,512]{1,0:T(8,128)(2,1)}, u32[]{:S(2)}, u32[]{:S(2)}) collective-permute-start(bf16[1024,512]{1,0:T(8,128)(2,1)S(1)} %get-tuple-element.46.refs_0_.refs_1_), channel_id=1, source_target_pairs={{0,8},{4,12},{8,0},{12,4},{1,9},{5,13},{9,1},{13,5},{2,10},{6,14},... | collective-permute-start | bytes 3145736 | tf_op jit(solution)/shard_map/ppermute | solution.py:268
  57.6 51.5 %collective-permute-start.9 = (bf16[2,1024,512]{2,1,0:T(8,128)(2,1)}, bf16[2,1024,512]{2,1,0:T(8,128)(2,1)}, u32[]{:S(2)}, u32[]{:S(2)}) collective-permute-start(bf16[2,1024,512]{2,1,0:T(8,128)(2,1)} %get-tuple-element.52), channel_id=1, source_target_pairs={{0,1},{3,2},{4,5},{7,6},{8,9},{11,10},{12,13},{15,14},{16,17},{19,... | collective-permute-start | bytes 6291464 | tf_op jit(solution)/shard_map/ppermute | solution.py:228
  64.1 48.1 %collective-permute-start.10 = (bf16[512,1536]{1,0:T(8,128)(2,1)}, bf16[512,1536]{1,0:T(8,128)(2,1)}, u32[]{:S(2)}, u32[]{:S(2)}) collective-permute-start(bf16[512,1536]{1,0:T(8,128)(2,1)} %collective-permute-done.3), channel_id=1, source_target_pairs={{1,0},{2,3},{5,4},{6,7},{9,8},{10,11},{13,12},{14,15},{17,16},{18,... | collective-permute-start | bytes 4718600 | tf_op jit(solution)/shard_map/ppermute | solution.py:228
  65.4 50.8 %collective-permute-start.11 = (bf16[512,1536]{1,0:T(8,128)(2,1)}, bf16[512,1536]{1,0:T(8,128)(2,1)S(1)}, u32[]{:S(2)}, u32[]{:S(2)}) collective-permute-start(bf16[512,1536]{1,0:T(8,128)(2,1)} %collective-permute-done.4.refs_13_), channel_id=1, source_target_pairs={{0,16},{16,0},{1,17},{17,1},{2,18},{18,2},{3,19},{19,3},{4,20},{20... | collective-permute-start | bytes 4718600 | tf_op jit(solution)/shard_map/ppermute | solution.py:231
  67.5 29.5 %collective-permute-start.12 = (bf16[1024,512]{1,0:T(8,128)(2,1)S(1)}, bf16[1024,512]{1,0:T(8,128)(2,1)S(1)}, u32[]{:S(2)}, u32[]{:S(2)}) collective-permute-start(bf16[1024,512]{1,0:T(8,128)(2,1)S(1)} %get-tuple-element.54.refs_0_.refs_2_), channel_id=1, source_target_pairs={{0,4},{4,0},{8,12},{12,8},{1,5},{5,1},{9,13},{13,9},{2,6},{6,2},{1... | collective-permute-start | bytes 3145736 | tf_op jit(solution)/shard_map/ppermute | solution.py:267
  91.5 63.4 %collective-permute-start.18 = (bf16[2,1024,512]{2,1,0:T(8,128)(2,1)}, bf16[2,1024,512]{2,1,0:T(8,128)(2,1)S(1)}, u32[]{:S(2)}, u32[]{:S(2)}) collective-permute-start(bf16[2,1024,512]{2,1,0:T(8,128)(2,1)} %get-tuple-element.62), channel_id=1, source_target_pairs={{0,1},{3,2},{4,5},{7,6},{8,9},{11,10},{12,13},{15,14},{16,17},{19,... | collective-permute-start | bytes 6291464 | tf_op jit(solution)/shard_map/ppermute | solution.py:228
  109.1 36.9 %collective-permute-start.16 = (bf16[512,1536]{1,0:T(8,128)(2,1)}, bf16[512,1536]{1,0:T(8,128)(2,1)}, u32[]{:S(2)}, u32[]{:S(2)}) collective-permute-start(bf16[512,1536]{1,0:T(8,128)(2,1)} %collective-permute-done.5), channel_id=1, source_target_pairs={{1,0},{2,3},{5,4},{6,7},{9,8},{10,11},{13,12},{14,15},{17,16},{18,... | collective-permute-start | bytes 4718600 | tf_op jit(solution)/shard_map/ppermute | solution.py:228
  116.3 36.2 %collective-permute-start.17 = (bf16[512,1536]{1,0:T(8,128)(2,1)S(1)}, bf16[512,1536]{1,0:T(8,128)(2,1)S(1)}, u32[]{:S(2)}, u32[]{:S(2)}) collective-permute-start(bf16[512,1536]{1,0:T(8,128)(2,1)S(1)} %add.73.refs_15_), channel_id=1, source_target_pairs={{0,16},{16,0},{1,17},{17,1},{2,18},{18,2},{3,19},{19,3},{4,20},{20... | collective-permute-start | bytes 4718600 | tf_op jit(solution)/shard_map/ppermute | solution.py:231
  128.6 74.3 %collective-permute-start.23 = (bf16[2,1024,512]{2,1,0:T(8,128)(2,1)}, bf16[2,1024,512]{2,1,0:T(8,128)(2,1)}, u32[]{:S(2)}, u32[]{:S(2)}) collective-permute-start(bf16[2,1024,512]{2,1,0:T(8,128)(2,1)} %get-tuple-element.71), channel_id=1, source_target_pairs={{0,1},{3,2},{4,5},{7,6},{8,9},{11,10},{12,13},{15,14},{16,17},{19,... | collective-permute-start | bytes 6291464 | tf_op jit(solution)/shard_map/ppermute | solution.py:228
  149.3 35.4 %collective-permute-start.20 = (bf16[512,1536]{1,0:T(8,128)(2,1)}, bf16[512,1536]{1,0:T(8,128)(2,1)}, u32[]{:S(2)}, u32[]{:S(2)}) collective-permute-start(bf16[512,1536]{1,0:T(8,128)(2,1)} %add.76.refs_17_), channel_id=1, source_target_pairs={{0,16},{16,0},{1,17},{17,1},{2,18},{18,2},{3,19},{19,3},{4,20},{20... | collective-permute-start | bytes 4718600 | tf_op jit(solution)/shard_map/ppermute | solution.py:231
  153.6 44.6 %collective-permute-start.21 = (bf16[1024,512]{1,0:T(8,128)(2,1)}, bf16[1024,512]{1,0:T(8,128)(2,1)}, u32[]{:S(2)}, u32[]{:S(2)}) collective-permute-start(bf16[1024,512]{1,0:T(8,128)(2,1)} %add_convert_fusion.9), channel_id=1, source_target_pairs={{1,0},{2,3},{5,4},{6,7},{9,8},{10,11},{13,12},{14,15},{17,16},{18,... | collective-permute-start | bytes 3145736 | tf_op jit(solution)/shard_map/ppermute | solution.py:228
  156.6 41.6 %collective-permute-start.22 = (bf16[1024,512]{1,0:T(8,128)(2,1)}, bf16[1024,512]{1,0:T(8,128)(2,1)}, u32[]{:S(2)}, u32[]{:S(2)}) collective-permute-start(bf16[1024,512]{1,0:T(8,128)(2,1)} %fusion.2), channel_id=1, source_target_pairs={{1,2},{2,1},{5,6},{6,5},{9,10},{10,9},{13,14},{14,13},{17,18},{18,... | collective-permute-start | bytes 3145736 | tf_op jit(solution)/shard_map/ppermute | solution.py:228
  158.3 71.8 %collective-permute-start.25 = (bf16[1024,512]{1,0:T(8,128)(2,1)}, bf16[1024,512]{1,0:T(8,128)(2,1)S(1)}, u32[]{:S(2)}, u32[]{:S(2)}) collective-permute-start(bf16[1024,512]{1,0:T(8,128)(2,1)} %copy-done.8), channel_id=1, source_target_pairs={{0,1},{3,2},{4,5},{7,6},{8,9},{11,10},{12,13},{15,14},{16,17},{19,... | collective-permute-start | bytes 3145736 | tf_op jit(solution)/shard_map/ppermute | solution.py:228
  199.9 32.6 %collective-permute-start.24 = (bf16[1024,512]{1,0:T(8,128)(2,1)S(1)}, bf16[1024,512]{1,0:T(8,128)(2,1)}, u32[]{:S(2)}, u32[]{:S(2)}) collective-permute-start(bf16[1024,512]{1,0:T(8,128)(2,1)S(1)} %add_convert_fusion.6), channel_id=1, source_target_pairs={{1,0},{2,3},{5,4},{6,7},{9,8},{10,11},{13,12},{14,15},{17,16},{18,... | collective-permute-start | bytes 3145736 | tf_op jit(solution)/shard_map/ppermute | solution.py:228
  201.2 32.9 %collective-permute-start.26 = (bf16[1024,512]{1,0:T(8,128)(2,1)S(1)}, bf16[1024,512]{1,0:T(8,128)(2,1)}, u32[]{:S(2)}, u32[]{:S(2)}) collective-permute-start(bf16[1024,512]{1,0:T(8,128)(2,1)S(1)} %fusion.3), channel_id=1, source_target_pairs={{1,2},{2,1},{5,6},{6,5},{9,10},{10,9},{13,14},{14,13},{17,18},{18,... | collective-permute-start | bytes 3145736 | tf_op jit(solution)/shard_map/ppermute | solution.py:228
  204.5 41.8 %collective-permute-start.27 = (bf16[1024,512]{1,0:T(8,128)(2,1)S(1)}, bf16[1024,512]{1,0:T(8,128)(2,1)S(1)}, u32[]{:S(2)}, u32[]{:S(2)}) collective-permute-start(bf16[1024,512]{1,0:T(8,128)(2,1)S(1)} %fusion.4), channel_id=1, source_target_pairs={{1,2},{2,1},{5,6},{6,5},{9,10},{10,9},{13,14},{14,13},{17,18},{18,... | collective-permute-start | bytes 3145736 | tf_op jit(solution)/shard_map/ppermute | solution.py:228
  205.2 46.8 %collective-permute-start.28 = (bf16[1024,512]{1,0:T(8,128)(2,1)S(1)}, bf16[1024,512]{1,0:T(8,128)(2,1)}, u32[]{:S(2)}, u32[]{:S(2)}) collective-permute-start(bf16[1024,512]{1,0:T(8,128)(2,1)S(1)} %copy-done.10), channel_id=1, source_target_pairs={{0,1},{3,2},{4,5},{7,6},{8,9},{11,10},{12,13},{15,14},{16,17},{19,... | collective-permute-start | bytes 3145736 | tf_op jit(solution)/shard_map/ppermute | solution.py:228
  230.1 37.0 %collective-permute-start.31 = (bf16[1024,512]{1,0:T(8,128)(2,1)S(1)}, bf16[1024,512]{1,0:T(8,128)(2,1)}, u32[]{:S(2)}, u32[]{:S(2)}) collective-permute-start(bf16[1024,512]{1,0:T(8,128)(2,1)S(1)} %copy-done.12), channel_id=1, source_target_pairs={{0,1},{3,2},{4,5},{7,6},{8,9},{11,10},{12,13},{15,14},{16,17},{19,... | collective-permute-start | bytes 3145736 | tf_op jit(solution)/shard_map/ppermute | solution.py:228
  246.6 27.0 %collective-permute-start.30 = (bf16[1024,512]{1,0:T(8,128)(2,1)S(1)}, bf16[1024,512]{1,0:T(8,128)(2,1)S(1)}, u32[]{:S(2)}, u32[]{:S(2)}) collective-permute-start(bf16[1024,512]{1,0:T(8,128)(2,1)S(1)} %add_convert_fusion.3), channel_id=1, source_target_pairs={{1,0},{2,3},{5,4},{6,7},{9,8},{10,11},{13,12},{14,15},{17,16},{18,... | collective-permute-start | bytes 3145736 | tf_op jit(solution)/shard_map/ppermute | solution.py:228
  248.0 25.5 %collective-permute-start.29 = (bf16[1024,512]{1,0:T(8,128)(2,1)S(1)}, bf16[1024,512]{1,0:T(8,128)(2,1)}, u32[]{:S(2)}, u32[]{:S(2)}) collective-permute-start(bf16[1024,512]{1,0:T(8,128)(2,1)S(1)} %fusion.5), channel_id=1, source_target_pairs={{1,2},{2,1},{5,6},{6,5},{9,10},{10,9},{13,14},{14,13},{17,18},{18,... | collective-permute-start | bytes 3145736 | tf_op jit(solution)/shard_map/ppermute | solution.py:228
  (33 other events, 491.7 us)

commit v3 on v2

--- a/solution.py
+++ b/solution.py
@@ -89,12 +89,12 @@
     )(*operands)
 
 
-def attention_backward(segments, qkv, grad_att, start, into):
+def attention_backward(segments, qkv, grad_att, start, into, count):
     tokens, width = qkv.shape[1:]
     block = 2 * HD
-    rows = grad_att.shape[0]
+    rows = count * LEN
     in_specs, operands = attention_specs(segments, qkv, start)
-    in_specs.append(pl.BlockSpec((LEN, block), lambda s, h: (s, h)))
+    in_specs.append(pl.BlockSpec((LEN, block), lambda s, h: (start + s, h)))
     operands.append(grad_att)
     if into is not None:
         in_specs.append(pl.BlockSpec(memory_space=pl.ANY))
@@ -112,14 +112,16 @@
 
 
 def partial_kernel(order, attended, *refs):
-    *features, pair, third, own, held = refs
+    *features, stack, rest, own, held = refs
     for at, block in enumerate(features):
         held[at] = dot(attended[...], block[...], NN)
-    for at, out in enumerate((pair.at[0], pair.at[1], third, own)):
-        out[...] = held[order[at]].astype(out.dtype)
-
-
-def partial_call(order, attended, features):
+    for at in range(stack.shape[0]):
+        stack[at] = held[order[at]].astype(stack.dtype)
+    rest[0] = held[order[2]].astype(rest.dtype)
+    own[...] = held[order[3]]
+
+
+def partial_call(order, attended, features, together):
     width, tokens = attended.shape
     chunk = features[0].shape[1]
     rows = min(256, width)
@@ -131,12 +133,16 @@
             grid=(width // rows,),
             in_specs=[pl.BlockSpec((rows, tokens), lambda r, _: (r, 0))]
             + [pl.BlockSpec((tokens, chunk), lambda r, _: (0, 0)) for _ in features],
-            out_specs=[pl.BlockSpec((2, rows, chunk), lambda r, _: (0, r, 0)), out, out],
+            out_specs=[
+                pl.BlockSpec((together, rows, chunk), lambda r, _: (0, r, 0)),
+                pl.BlockSpec((1, rows, chunk), lambda r, _: (0, r, 0)),
+                out,
+            ],
             scratch_shapes=[pltpu.VMEM((len(features), rows, chunk), jnp.float32)],
         ),
         out_shape=[
-            jax.ShapeDtypeStruct((2, width, chunk), jnp.bfloat16),
-            jax.ShapeDtypeStruct((width, chunk), jnp.bfloat16),
+            jax.ShapeDtypeStruct((together, width, chunk), jnp.bfloat16),
+            jax.ShapeDtypeStruct((1, width, chunk), jnp.bfloat16),
             jax.ShapeDtypeStruct((width, chunk), jnp.float32),
         ],
         compiler_params=ROOM,
@@ -147,54 +153,64 @@
     )(order, attended, *features)
 
 
-def attended_kernel(order, *refs):
-    *features, own, one, one_far, two, two_far, three, three_far, out, held = refs
-    blocks = held.shape[0]
-    pieces = len(features) // blocks
-    half = one.shape[0]
+def attended_kernel(blocks, slots, order, *refs):
+    *operands, out, held = refs
+    pieces = (len(operands) - 2 * len(slots) - 1) // blocks
+    features, start_value = operands[: blocks * pieces], operands[blocks * pieces]
+    weights = operands[blocks * pieces + 1 :]
+    half = weights[0].shape[0]
     for at in range(blocks):
         start = 0
         for piece in features[at * pieces : (at + 1) * pieces]:
             stop = start + piece.shape[1]
             held[at, :, start:stop] = piece[...]
             start = stop
-    near_start = pl.multiple_of(order[4] * half, HD)
-    far_start = pl.multiple_of((1 - order[4]) * half, HD)
-    near = dot(held[order[0]], own[pl.ds(near_start, half), :], NT)
-    far = dot(held[order[0]], own[pl.ds(far_start, half), :], NT)
-    for slot, (here, there) in enumerate(((one, one_far), (two, two_far), (three, three_far))):
-        near += dot(held[order[slot + 1]], here[...], NT)
-        far += dot(held[order[slot + 1]], there[...], NT)
-    out[:, pl.ds(near_start, half)] = near.astype(jnp.bfloat16)
-    out[:, pl.ds(far_start, half)] = far.astype(jnp.bfloat16)
-
-
-def attended_call(order, gathered, weights, start, tokens):
-    width, own_width = weights[0].shape
+    near = pl.ds(pl.multiple_of(order[4] * half, HD), half)
+    far = pl.ds(pl.multiple_of((1 - order[4]) * half, HD), half)
+    for side, columns in enumerate((near, far)):
+        if 1 in slots:
+            total = dot(held[order[0]], start_value[columns, :], NT)
+        else:
+            total = start_value[:, columns]
+        for at, slot in enumerate(slots):
+            total += dot(held[order[slot]], weights[2 * at + side][...], NT)
+        out[:, columns] = total.astype(out.dtype)
+
+
+def attended_call(order, gathered, slots, start_value, weights, kind):
+    features = [pieces[at] for at in range(len(gathered[0])) for pieces in gathered]
     blocks = len(gathered[0])
-    features = [pieces[at] for at in range(blocks) for pieces in gathered]
+    tokens = features[0].shape[0]
+    own_width = weights[0].shape[1]
+    width = 2 * weights[0].shape[0]
     rows = min(256, tokens)
-    skip = start // rows
+    whole = [
+        pl.BlockSpec(w.shape, lambda r, _: (0, 0), pipeline_mode=pl.Buffered(1)) for w in weights
+    ]
+    if 1 in slots:
+        first = pl.BlockSpec(
+            start_value.shape, lambda r, _: (0, 0), pipeline_mode=pl.Buffered(1)
+        )
+    else:
+        first = pl.BlockSpec((rows, width), lambda r, _: (r, 0))
     return pl.pallas_call(
-        attended_kernel,
+        functools.partial(attended_kernel, blocks, slots),
         grid_spec=pltpu.PrefetchScalarGridSpec(
             num_scalar_prefetch=1,
             grid=(tokens // rows,),
-            in_specs=[pl.BlockSpec((rows, f.shape[1]), lambda r, _: (skip + r, 0)) for f in features]
-            + [
-                pl.BlockSpec(w.shape, lambda r, _: (0, 0), pipeline_mode=pl.Buffered(1))
-                for w in weights
-            ],
+            in_specs=[pl.BlockSpec((rows, f.shape[1]), lambda r, _: (r, 0)) for f in features]
+            + [first]
+            + whole,
             out_specs=pl.BlockSpec((rows, width), lambda r, _: (r, 0)),
             scratch_shapes=[pltpu.VMEM((blocks, rows, own_width), jnp.bfloat16)],
         ),
-        out_shape=jax.ShapeDtypeStruct((tokens, width), jnp.bfloat16),
+        out_shape=jax.ShapeDtypeStruct((tokens, width), kind),
         compiler_params=ROOM,
         cost_estimate=cost(
-            2 * tokens * width * blocks * own_width,
-            2 * (blocks * own_width * (tokens + width) + tokens * width),
+            2 * tokens * width * own_width * len(slots),
+            2 * (blocks * own_width * (tokens + width) + 2 * tokens * width),
         ),
-    )(order, *features, *weights)
+    )(order, *features, start_value, *weights)
 
 
 def plain_shards(qkv, grad_out, out_weight, segments):
@@ -204,7 +220,7 @@
     block = dot(attended, rows, NN)
     grad_weight = lax.psum_scatter(block, "dp", scatter_dimension=1, tiled=True)
     grad_att = dot(rows, projection, NT).astype(jnp.bfloat16)
-    grad_qkv = attention_backward(segments, qkv, grad_att, 0, None)
+    grad_qkv = attention_backward(segments, qkv, grad_att, 0, None, qkv.shape[1] // LEN)
     return grad_qkv, grad_weight.astype(jnp.bfloat16)
 
 
@@ -217,7 +233,7 @@
 def shards(qkv, grad_out, out_weight, segments):
     width = qkv.shape[2]
     own_width = grad_out.shape[1]
-    chunk = own_width // CHUNKS
+    starts = [0, 5 * own_width // 12, 2 * own_width // 3, own_width]
     group = lax.axis_index("groups")
     here = lax.axis_index("mp")
     place = lax.axis_index("dp")
@@ -244,9 +260,7 @@
     first = along(own_half, OUTER)
     middle = along(own_half, MIDDLE)
     first_far = swap_groups(first)
-    middle_second = along(first, MIDDLE)
     outward = along(middle, OUTWARD)
-    outward_second = along(middle_second, OUTWARD)
 
     attended = done(attention_forward(segments, qkv))
 
@@ -261,7 +275,7 @@
     gathered, partials = [], []
 
     def gather(c):
-        mine = grad_out[:, c * chunk : (c + 1) * chunk].astype(jnp.bfloat16)
+        mine = grad_out[:, starts[c] : starts[c + 1]].astype(jnp.bfloat16)
         if c:
             mine = after(mine, attended)
         near = lax.ppermute(mine, "mp", [(i, i ^ 1) for i in range(4)])
@@ -271,10 +285,10 @@
 
     def partial(c, *others):
         partials.append(
-            done(*partial_call(chained(partial_order, *others), attended, gathered[c]))
+            done(*partial_call(chained(partial_order, *others), attended, gathered[c], 3 if c == 1 else 2))
         )
 
-    pairs_in, last_in, middle_sums, outward_sums = [], [], [], []
+    pairs_in, last_in, middle_sums, outward_sums = [], {}, [], []
 
     def send_pair(c, *others):
         value = partials[c][0]
@@ -283,7 +297,7 @@
         pairs_in.append(along(value, INWARD))
 
     def send_last(c, *others):
-        last_in.append(along(after(partials[c][1], *others), INWARD))
+        last_in[c] = along(after(partials[c][1][0], *others), INWARD)
 
     def send_middle(t, c, *others):
         mine, arrived = chained(partials[c][0], *others)[t], pairs_in[c][t]
@@ -292,7 +306,7 @@
 
     def send_outward(c, *others):
         arrived = middle_sums[2 * c]
-        value = chained(partials[c][1], *others).astype(jnp.float32)
+        value = chained(partials[c][1][0], *others).astype(jnp.float32)
         value = value + arrived.astype(jnp.float32)
         outward_sums.append(along(done(value.astype(jnp.bfloat16)), OUTWARD))
 
@@ -308,27 +322,37 @@
     ).astype(jnp.int32)
     grad_att = []
 
-    def attended_gradient(s, *others):
-        weights = [out_weight, first, first_far, second, second_far, third, third_far]
-        found = attended_call(chained(attended_order, *others), gathered, weights, s * LEN, LEN)
-        grad_att.append(done(found))
+    def attended_gradient(slots, start_value, weights, kind, *others):
+        grad_att.append(
+            done(
+                attended_call(
+                    chained(attended_order, *others), gathered, slots, start_value, weights, kind
+                )
+            )
+        )
 
     def backward(s, *others):
         grads.append(
-            done(attention_backward(segments, qkv, chained(grad_att[s], *others), s, grads[-1]))
+            done(
+                attention_backward(
+                    segments, qkv, chained(grad_att[1], *others), s, grads[-1], 1
+                )
+            )
         )
 
     def finish(c, into):
         total = chained(partials[c][2])
-        for part in (middle_sums[2 * c + 1], outward_sums[c], last_in[c]):
+        for part in (middle_sums[2 * c + 1], outward_sums[c], last_in.get(c, pairs_in[1][-1])):
             total = total + part.astype(jnp.float32)
         return done(
-            lax.dynamic_update_slice_in_dim(into, total.astype(jnp.bfloat16), c * chunk, 1)
+            lax.dynamic_update_slice_in_dim(into, total.astype(jnp.bfloat16), starts[c], 1)
         )
 
     gather(0)
     partial(0)
     send_pair(0, first, middle)
+    middle_second = along(after(first, partials[0][0]), MIDDLE)
+    outward_second = along(middle_second, OUTWARD)
     gather(1)
     partial(1, middle_second)
     gather(2)
@@ -345,18 +369,18 @@
     send_middle(0, 1, second_far)
     send_last(0, pairs_in[1])
     send_middle(1, 1, middle_sums[1])
-    attended_gradient(0)
+    near_weights = [first, first_far, second, second_far]
+    attended_gradient((1, 2), out_weight, near_weights, jnp.float32)
     send_outward(1, outward_sums[0])
-    send_middle(0, 2)
-    attended_gradient(1)
-    send_last(1, pairs_in[1])
-    send_middle(1, 2, outward_sums[1], last_in[0])
-    backward(0, middle_sums[3])
-    send_outward(2)
+    attended_gradient((3,), grad_att[0], [third, third_far], jnp.bfloat16)
+    send_middle(0, 2, middle_sums[3])
+    send_middle(1, 2)
+    backward(0)
+    send_outward(2, last_in[0], outward_sums[1])
     grad_weight = jnp.zeros((width, own_width), jnp.bfloat16)
     grad_weight = finish(0, grad_weight)
     send_last(2, pairs_in[2])
-    backward(1, last_in[1])
+    backward(1)
     grad_weight = finish(1, grad_weight)
     grad_weight = finish(2, grad_weight)
     return grads[-1], grad_weight

time: 279 us -> 277 us (level)
  starting transfers between devices: 87.7 us -> 81 us
  local copies, waits for them, and re-layouts: 9.69 us -> 12.8 us
  Pallas kernels: 90.2 us -> 93.2 us
    ppermute x20 -> x19, waiting for transfers between devices: 39.3 us -> 15.7 us  [along(): return lax.ppermute(array, 'dp', pairs)]
    ppermute x3, waiting for transfers between devices: 16.1 us -> 37.9 us  [gather(): across = lax.ppermute(mine, 'mp', [(i, i ^ 2) for i in range(4)])]
    ppermute x20 -> x19, starting transfers between devices: 77 us -> 70 us  [along(): return lax.ppermute(array, 'dp', pairs)]
    unnamed x50 -> x74, local copies, waits for them, and re-layouts: 5.38 us -> 9.31 us
    ppermute x3, waiting for transfers between devices: 0.01 us -> 3.09 us  [gather(): both = lax.ppermute(chained(across), 'mp', [(i, i ^ 1) for i in range(4)])]
  transfers between devices with their start and end apart: 32 -> 31, of which waited for: 7 -> 6; matrix products, arithmetic and copies ran while one was open for 11% -> 11% of each run, Pallas kernels for 33% -> 34%
where the time goes in v3:
time: 277 us; the launch traced here: 276 us
  Pallas kernels  93.2 us (34%)
  starting transfers between devices  81 us (29%)
  waiting for transfers between devices  56.7 us (20%)
  other arithmetic  30.7 us (11%)
  local copies, waits for them, and re-layouts  12.8 us (5%)
    ppermute x19, starting transfers between devices, along(): return lax.ppermute(array, 'dp', pairs)  70 us
    ppermute x3, waiting for transfers between devices, gather(): across = lax.ppermute(mine, 'mp', [(i, i ^ 2) for i in range(4)])  37.9 us
    pallas_call x2, Pallas kernels, attended_call(): pl.pallas_call(functools.partial(attended_kernel, blocks, slots), grid_sp...  27.7 us
    pallas_call x3, Pallas kernels, partial_call(): pl.pallas_call(partial_kernel, grid_spec=pltpu.PrefetchScalarGridSpec(num...  27.6 us
    pallas_call x2, Pallas kernels, attention_backward(): pl.pallas_call(backward_kernel, grid=(rows // LEN, width // block), in_sp...  24.6 us
    ppermute x19, waiting for transfers between devices, along(): return lax.ppermute(array, 'dp', pairs)  15.7 us
    pallas_call x1, Pallas kernels, attention_forward(): pl.pallas_call(forward_kernel, grid=(tokens // LEN, width // block), in_s...  13.3 us
    convert_element_type x6, other arithmetic, send_middle(): middle_sums.append(along(done(value.astype(jnp.bfloat16)), MIDDLE))  12.1 us
  transfers between devices with their start and end apart: 31, of which 6 were waited for; matrix products, arithmetic and copies ran while one was open for 11% of the time, Pallas kernels for 34%

profile of v3, /device:TPU:0, one launch (start us, length us, event | category | flops | bytes accessed | tf_op | source)
XLA Modules:
  0.0 275.5 jit_solution(12177881021480468995)
XLA Ops:
  0.6 3.2 %convert.6 = bf16[1024,1536]{1,0:T(8,128)(2,1)S(1)} convert(f32[1024,1536]{1,0:T(8,128)} %param.5) | non-fusion elementwise | flops 1572864 | bytes 9437184 | tf_op jit(solution)/shard_map/convert.3
  5.6 3.0 %collective-permute-start.1 = (bf16[1024,640]{1,0:T(8,128)(2,1)S(1)}, bf16[1024,640]{1,0:T(8,128)(2,1)S(1)}, u32[]{:S(2)}, u32[]{:S(2)}) collective-permute-start(bf16[1024,640]{1,0:T(8,128)(2,1)S(1)} %slice.67.refs_0_), channel_id=1, source_target_pairs={{0,8},{4,12},{8,0},{12,4},{1,9},{5,13},{9,1},{13,5},{2,10},{6,14},... | collective-permute-start | bytes 3932168 | tf_op jit(solution)/shard_map/ppermute | solution.py:282
  14.9 13.3 %shard_map.59.attended = bf16[1024,1024]{1,0:T(8,128)(2,1)S(1)} custom-call(s32[2,512,1]{2,1,0:T(8,128)S(1)} %copy.9.column_ids, s32[2,1,512]{2,1,0:T(1,128)S(1)} %reshape.41.row_ids, bf16[3,1024,1024]{2,1,0:T(8,128)(2,1)} %qkv.5), custom_call_target="tpu_custom_call" | custom-call | flops 107374184 | bytes 419430 | tf_op jit(solution)/shard_map/pallas_call | solution.py:81
  29.6 7.8 %collective-permute-done.1.refs_2_.refs_6_ = bf16[1024,640]{1,0:T(8,128)(2,1)S(1)} collective-permute-done((bf16[1024,640]{1,0:T(8,128)(2,1)S(1)}, bf16[1024,640]{1,0:T(8,128)(2,1)S(1)}, u32[]{:S(2)}, u32[]{:S(2)}) %collective-permute-start.1) | collective-permute-done | bytes 1310752 | tf_op jit(solution)/shard_map/ppermute | solution.py:282
  37.5 3.1 %collective-permute-done.2.refs_3_.refs_9_ = bf16[1024,640]{1,0:T(8,128)(2,1)} collective-permute-done((bf16[1024,640]{1,0:T(8,128)(2,1)S(1)}, bf16[1024,640]{1,0:T(8,128)(2,1)}, u32[]{:S(2)}, u32[]{:S(2)}) %collective-permute-start.2) | collective-permute-done | bytes 1310752 | tf_op jit(solution)/shard_map/ppermute | solution.py:283
  40.6 11.5 %shard_map.60 = (bf16[2,1024,640]{2,1,0:T(8,128)(2,1)}, bf16[1,1024,640]{2,1,0:T(8,128)(2,1)S(1)}, f32[1024,640]{1,0:T(8,128)}) custom-call(s32[4]{0:T(128)S(1)} %pad_add_fusion.order, bf16[1024,1024]{1,0:T(8,128)(2,1)} %copy-done, bf16[1024,640]{1,0:T(8,128)(2,1)S(1)} %slice.67.refs_0_, bf16[1024,640]{1,0:T(8,128)(2,1)} %collective-permute-done.refs_1_.refs_3_, ...), custom_call_target="tpu_custom_call" | custom-call | flops 268435456 | bytes 629145 | tf_op jit(solution)/shard_map/pallas_call | solution.py:129
  52.1 5.2 %collective-permute-start.9 = (bf16[2,1024,640]{2,1,0:T(8,128)(2,1)}, bf16[2,1024,640]{2,1,0:T(8,128)(2,1)}, u32[]{:S(2)}, u32[]{:S(2)}) collective-permute-start(bf16[2,1024,640]{2,1,0:T(8,128)(2,1)} %get-tuple-element.55), channel_id=1, source_target_pairs={{0,1},{3,2},{4,5},{7,6},{8,9},{11,10},{12,13},{15,14},{16,17},{19,... | collective-permute-start | bytes 7864328 | tf_op jit(solution)/shard_map/ppermute | solution.py:244
  59.8 17.0 %collective-permute-done.6.refs_2_.refs_7_ = bf16[1024,384]{1,0:T(8,128)(2,1)S(1)} collective-permute-done((bf16[1024,384]{1,0:T(8,128)(2,1)S(1)}, bf16[1024,384]{1,0:T(8,128)(2,1)S(1)}, u32[]{:S(2)}, u32[]{:S(2)}) %collective-permute-start.6) | collective-permute-done | bytes 786464 | tf_op jit(solution)/shard_map/ppermute | solution.py:282
  81.3 8.0 %shard_map.61 = (bf16[3,1024,384]{2,1,0:T(8,128)(2,1)}, bf16[1,1024,384]{2,1,0:T(8,128)(2,1)S(1)}, f32[1024,384]{1,0:T(8,128)S(1)}) custom-call(s32[4]{0:T(128)S(1)} %pad_add_fusion.order, bf16[1024,1024]{1,0:T(8,128)(2,1)} %copy-done, bf16[1024,384]{1,0:T(8,128)(2,1)S(1)} %slice.68.refs_0_.refs_1_, ...), custom_call_target="tpu_custom_call" | custom-call | flops 161061280 | bytes 419430 | tf_op jit(solution)/shard_map/pallas_call | solution.py:129
  89.4 13.1 %collective-permute-done.13.refs_2_.refs_8_ = bf16[1024,512]{1,0:T(8,128)(2,1)S(1)} collective-permute-done((bf16[1024,512]{1,0:T(8,128)(2,1)S(1)}, bf16[1024,512]{1,0:T(8,128)(2,1)S(1)}, u32[]{:S(2)}, u32[]{:S(2)}) %collective-permute-start.13) | collective-permute-done | bytes 1048608 | tf_op jit(solution)/shard_map/ppermute | solution.py:282
  102.5 4.0 %collective-permute-start.18 = (bf16[3,1024,384]{2,1,0:T(8,128)(2,1)}, bf16[3,1024,384]{2,1,0:T(8,128)(2,1)}, u32[]{:S(2)}, u32[]{:S(2)}) collective-permute-start(bf16[3,1024,384]{2,1,0:T(8,128)(2,1)} %get-tuple-element.63), channel_id=1, source_target_pairs={{0,1},{3,2},{4,5},{7,6},{8,9},{11,10},{12,13},{15,14},{16,17},{19,... | collective-permute-start | bytes 7077896 | tf_op jit(solution)/shard_map/ppermute | solution.py:244
  106.6 6.8 %collective-permute-done.9 = bf16[2,1024,640]{2,1,0:T(8,128)(2,1)} collective-permute-done((bf16[2,1024,640]{2,1,0:T(8,128)(2,1)}, bf16[2,1024,640]{2,1,0:T(8,128)(2,1)}, u32[]{:S(2)}, u32[]{:S(2)}) %collective-permute-start.9) | collective-permute-done | bytes 2621472 | tf_op jit(solution)/shard_map/ppermute | solution.py:244
  113.3 2.7 fusion.1
  125.5 8.1 %shard_map.62 = (bf16[2,1024,512]{2,1,0:T(8,128)(2,1)}, bf16[1,1024,512]{2,1,0:T(8,128)(2,1)S(1)}, f32[1024,512]{1,0:T(8,128)}) custom-call(s32[4]{0:T(128)S(1)} %pad_add_fusion.order, bf16[1024,1024]{1,0:T(8,128)(2,1)} %copy-done, bf16[1024,512]{1,0:T(8,128)(2,1)S(1)} %slice.71.refs_0_.refs_2_, ...), custom_call_target="tpu_custom_call" | custom-call | flops 214748368 | bytes 524288 | tf_op jit(solution)/shard_map/pallas_call | solution.py:129
  133.7 22.0 %collective-permute-start.24 = (bf16[2,1024,512]{2,1,0:T(8,128)(2,1)}, bf16[2,1024,512]{2,1,0:T(8,128)(2,1)}, u32[]{:S(2)}, u32[]{:S(2)}) collective-permute-start(bf16[2,1024,512]{2,1,0:T(8,128)(2,1)} %get-tuple-element.71), channel_id=1, source_target_pairs={{0,1},{3,2},{4,5},{7,6},{8,9},{11,10},{12,13},{15,14},{16,17},{19,... | collective-permute-start | bytes 6291464 | tf_op jit(solution)/shard_map/ppermute | solution.py:244
  155.7 2.8 %add_convert_fusion.1 = bf16[1024,640]{1,0:T(8,128)(2,1)} fusion(bf16[1024,640]{1,0:T(8,128)(2,1)} %collective-permute-done.15, bf16[1024,640]{1,0:T(8,128)(2,1)S(1)} %bitcast.27), kind=kLoop, calls=%fused_computation.1 | loop fusion | flops 2621440 | bytes 3932160 | tf_op jit(solution)/shard_map/convert_element_type | solution.py:311
  159.8 3.1 %add.76.refs_13_ = bf16[512,1536]{1,0:T(8,128)(2,1)} add(bf16[512,1536]{1,0:T(8,128)(2,1)S(1)} %collective-permute-done.4, bf16[512,1536]{1,0:T(8,128)(2,1)} %collective-permute-done.16) | non-fusion elementwise | flops 786432 | bytes 4718592 | tf_op jit(solution)/shard_map/add | solution.py:367
  176.7 17.4 %shard_map.63.refs_12_ = f32[1024,1024]{1,0:T(8,128)} custom-call(s32[5]{0:T(128)S(1)} %stack.32.order, bf16[1024,640]{1,0:T(8,128)(2,1)} %copy-done.1, bf16[1024,384]{1,0:T(8,128)(2,1)S(1)} %slice.68.refs_0_.refs_1_, bf16[1024,512]{1,0:T(8,128)(2,1)S(1)} %slice.71.refs_0_.refs_2_, bf16[1024,640]{1,0:T(8,128)(2,1)} %collective-permute-done.refs_1_.refs_3_, ...), custom_call_target="tpu_custom_call" | custom-call | flops 322122560 | bytes 1468006 | tf_op jit(solution)/shard_map/pallas_call | solution.py:196
  194.2 16.1 %collective-permute-start.25 = (bf16[1024,640]{1,0:T(8,128)(2,1)S(1)}, bf16[1024,640]{1,0:T(8,128)(2,1)S(1)}, u32[]{:S(2)}, u32[]{:S(2)}) collective-permute-start(bf16[1024,640]{1,0:T(8,128)(2,1)S(1)} %bitcast.28), channel_id=1, source_target_pairs={{0,1},{3,2},{4,5},{7,6},{8,9},{11,10},{12,13},{15,14},{16,17},{19,... | collective-permute-start | bytes 3932168 | tf_op jit(solution)/shard_map/ppermute | solution.py:244
  212.5 10.3 %shard_map.64.grad_att = bf16[1024,1024]{1,0:T(8,128)(2,1)} custom-call(s32[5]{0:T(128)S(1)} %stack.32.order, bf16[1024,640]{1,0:T(8,128)(2,1)} %copy-done.1, bf16[1024,384]{1,0:T(8,128)(2,1)S(1)} %slice.68.refs_0_.refs_1_, bf16[1024,512]{1,0:T(8,128)(2,1)S(1)} %slice.71.refs_0_.refs_2_, bf16[1024,640]{1,0:T(8,128)(2,1)} %collective-permute-done.refs_1_.refs_3_, ...), custom_call_target="tpu_custom_call" | custom-call | flops 161061280 | bytes 1468006 | tf_op jit(solution)/shard_map/pallas_call | solution.py:196
  226.7 4.7 %collective-permute-start.30 = (bf16[1024,512]{1,0:T(8,128)(2,1)S(1)}, bf16[1024,512]{1,0:T(8,128)(2,1)S(1)}, u32[]{:S(2)}, u32[]{:S(2)}) collective-permute-start(bf16[1024,512]{1,0:T(8,128)(2,1)S(1)} %bitcast.29), channel_id=1, source_target_pairs={{0,1},{3,2},{4,5},{7,6},{8,9},{11,10},{12,13},{15,14},{16,17},{19,... | collective-permute-start | bytes 3145736 | tf_op jit(solution)/shard_map/ppermute | solution.py:244
  233.7 12.3 %shard_map.65.refs_0_ = bf16[3,1024,1024]{2,1,0:T(8,128)(2,1)} custom-call(s32[2,512,1]{2,1,0:T(8,128)S(1)} %copy-done.9, s32[2,1,512]{2,1,0:T(1,128)S(1)} %reshape.41.row_ids, bf16[3,1024,1024]{2,1,0:T(8,128)(2,1)} %qkv.5, bf16[1024,1024]{1,0:T(8,128)(2,1)S(1)} %copy-done.2), custom_call_target="tpu_custom_call" | custom-call | flops 134217728 | bytes 367001 | tf_op jit(solution)/shard_map/pallas_call | solution.py:102
  250.0 12.3 %shard_map.66 = bf16[3,1024,1024]{2,1,0:T(8,128)(2,1)} custom-call(s32[2,512,1]{2,1,0:T(8,128)S(1)} %copy-done.9, s32[2,1,512]{2,1,0:T(1,128)S(1)} %reshape.41.row_ids, bf16[3,1024,1024]{2,1,0:T(8,128)(2,1)} %qkv.5, bf16[1024,1024]{1,0:T(8,128)(2,1)S(1)} %copy-done.2, bf16[3,1024,1024]{2,1,0:T(8,128)(2,1)} %shard_map.65.refs_0_), custom_call_target="tpu_custom_call", output_to_operand_aliasing={{}: (4, {})} | custom-call | flops 134217728 | bytes 367001 | tf_op jit(solution)/shard_map/pallas_call | solution.py:102
  264.4 8.9 %collective-permute-done.29 = bf16[1024,512]{1,0:T(8,128)(2,1)S(1)} collective-permute-done((bf16[1024,512]{1,0:T(8,128)(2,1)S(1)}, bf16[1024,512]{1,0:T(8,128)(2,1)S(1)}, u32[]{:S(2)}, u32[]{:S(2)}) %collective-permute-start.29) | collective-permute-done | bytes 1048608 | tf_op jit(solution)/shard_map/ppermute | solution.py:244
  (144 shorter events, 57.8 us)
Async XLA Ops:
  5.6 31.8 %collective-permute-start.1 = (bf16[1024,640]{1,0:T(8,128)(2,1)S(1)}, bf16[1024,640]{1,0:T(8,128)(2,1)S(1)}, u32[]{:S(2)}, u32[]{:S(2)}) collective-permute-start(bf16[1024,640]{1,0:T(8,128)(2,1)S(1)} %slice.67.refs_0_), channel_id=1, source_target_pairs={{0,8},{4,12},{8,0},{12,4},{1,9},{5,13},{9,1},{13,5},{2,10},{6,14},... | collective-permute-start | bytes 3932168 | tf_op jit(solution)/shard_map/ppermute | solution.py:282
  11.3 40.8 %collective-permute-start.3 = (bf16[512,1536]{1,0:T(8,128)(2,1)}, bf16[512,1536]{1,0:T(8,128)(2,1)}, u32[]{:S(2)}, u32[]{:S(2)}) collective-permute-start(bf16[512,1536]{1,0:T(8,128)(2,1)} %constant_dynamic-slice_fusion), channel_id=1, source_target_pairs={{0,1},{1,0},{2,3},{3,2},{4,5},{5,4},{6,7},{7,6},{8,9},{9,8},{10,11... | collective-permute-start | bytes 4718600 | tf_op jit(solution)/shard_map/ppermute | solution.py:244
  12.9 39.2 %collective-permute-start.8 = (bf16[512,1536]{1,0:T(8,128)(2,1)}, bf16[512,1536]{1,0:T(8,128)(2,1)}, u32[]{:S(2)}, u32[]{:S(2)}) collective-permute-start(bf16[512,1536]{1,0:T(8,128)(2,1)} %constant_dynamic-slice_fusion), channel_id=1, source_target_pairs={{1,2},{2,1},{5,6},{6,5},{9,10},{10,9},{13,14},{14,13},{17,18},{18,... | collective-permute-start | bytes 4718600 | tf_op jit(solution)/shard_map/ppermute | solution.py:244
  14.7 22.8 %collective-permute-start = (bf16[1024,640]{1,0:T(8,128)(2,1)S(1)}, bf16[1024,640]{1,0:T(8,128)(2,1)}, u32[]{:S(2)}, u32[]{:S(2)}) collective-permute-start(bf16[1024,640]{1,0:T(8,128)(2,1)S(1)} %slice.67.refs_0_), channel_id=1, source_target_pairs={{0,4},{4,0},{8,12},{12,8},{1,5},{5,1},{9,13},{13,9},{2,6},{6,2},{1... | collective-permute-start | bytes 3932168 | tf_op jit(solution)/shard_map/ppermute | solution.py:281
  52.1 61.3 %collective-permute-start.9 = (bf16[2,1024,640]{2,1,0:T(8,128)(2,1)}, bf16[2,1024,640]{2,1,0:T(8,128)(2,1)}, u32[]{:S(2)}, u32[]{:S(2)}) collective-permute-start(bf16[2,1024,640]{2,1,0:T(8,128)(2,1)} %get-tuple-element.55), channel_id=1, source_target_pairs={{0,1},{3,2},{4,5},{7,6},{8,9},{11,10},{12,13},{15,14},{16,17},{19,... | collective-permute-start | bytes 7864328 | tf_op jit(solution)/shard_map/ppermute | solution.py:244
  59.0 22.4 %collective-permute-start.4 = (bf16[512,1536]{1,0:T(8,128)(2,1)}, bf16[512,1536]{1,0:T(8,128)(2,1)S(1)}, u32[]{:S(2)}, u32[]{:S(2)}) collective-permute-start(bf16[512,1536]{1,0:T(8,128)(2,1)} %collective-permute-done.3.refs_13_), channel_id=1, source_target_pairs={{1,2},{2,1},{5,6},{6,5},{9,10},{10,9},{13,14},{14,13},{17,18},{18,... | collective-permute-start | bytes 4718600 | tf_op jit(solution)/shard_map/ppermute | solution.py:244
  76.9 25.6 %collective-permute-start.13 = (bf16[1024,512]{1,0:T(8,128)(2,1)S(1)}, bf16[1024,512]{1,0:T(8,128)(2,1)S(1)}, u32[]{:S(2)}, u32[]{:S(2)}) collective-permute-start(bf16[1024,512]{1,0:T(8,128)(2,1)S(1)} %slice.71.refs_0_.refs_2_), channel_id=1, source_target_pairs={{0,8},{4,12},{8,0},{12,4},{1,9},{5,13},{9,1},{13,5},{2,10},{6,14},... | collective-permute-start | bytes 3145736 | tf_op jit(solution)/shard_map/ppermute | solution.py:282
  78.4 39.4 %collective-permute-start.10 = (bf16[512,1536]{1,0:T(8,128)(2,1)}, bf16[512,1536]{1,0:T(8,128)(2,1)}, u32[]{:S(2)}, u32[]{:S(2)}) collective-permute-start(bf16[512,1536]{1,0:T(8,128)(2,1)} %collective-permute-done.8), channel_id=1, source_target_pairs={{1,0},{2,3},{5,4},{6,7},{9,8},{10,11},{13,12},{14,15},{17,16},{18,... | collective-permute-start | bytes 4718600 | tf_op jit(solution)/shard_map/ppermute | solution.py:244
  79.7 41.7 %collective-permute-start.11 = (bf16[512,1536]{1,0:T(8,128)(2,1)}, bf16[512,1536]{1,0:T(8,128)(2,1)S(1)}, u32[]{:S(2)}, u32[]{:S(2)}) collective-permute-start(bf16[512,1536]{1,0:T(8,128)(2,1)} %collective-permute-done.3.refs_13_), channel_id=1, source_target_pairs={{0,16},{16,0},{1,17},{17,1},{2,18},{18,2},{3,19},{19,3},{4,20},{20... | collective-permute-start | bytes 4718600 | tf_op jit(solution)/shard_map/ppermute | solution.py:247
  81.3 34.8 %collective-permute-start.12 = (bf16[1024,512]{1,0:T(8,128)(2,1)S(1)}, bf16[1024,512]{1,0:T(8,128)(2,1)S(1)}, u32[]{:S(2)}, u32[]{:S(2)}) collective-permute-start(bf16[1024,512]{1,0:T(8,128)(2,1)S(1)} %slice.71.refs_0_.refs_2_), channel_id=1, source_target_pairs={{0,4},{4,0},{8,12},{12,8},{1,5},{5,1},{9,13},{13,9},{2,6},{6,2},{1... | collective-permute-start | bytes 3145736 | tf_op jit(solution)/shard_map/ppermute | solution.py:281
  102.5 62.0 %collective-permute-start.18 = (bf16[3,1024,384]{2,1,0:T(8,128)(2,1)}, bf16[3,1024,384]{2,1,0:T(8,128)(2,1)}, u32[]{:S(2)}, u32[]{:S(2)}) collective-permute-start(bf16[3,1024,384]{2,1,0:T(8,128)(2,1)} %get-tuple-element.63), channel_id=1, source_target_pairs={{0,1},{3,2},{4,5},{7,6},{8,9},{11,10},{12,13},{15,14},{16,17},{19,... | collective-permute-start | bytes 7077896 | tf_op jit(solution)/shard_map/ppermute | solution.py:244
  117.8 40.6 %collective-permute-start.16 = (bf16[512,1536]{1,0:T(8,128)(2,1)S(1)}, bf16[512,1536]{1,0:T(8,128)(2,1)}, u32[]{:S(2)}, u32[]{:S(2)}) collective-permute-start(bf16[512,1536]{1,0:T(8,128)(2,1)S(1)} %collective-permute-done.4), channel_id=1, source_target_pairs={{1,0},{2,3},{5,4},{6,7},{9,8},{10,11},{13,12},{14,15},{17,16},{18,... | collective-permute-start | bytes 4718600 | tf_op jit(solution)/shard_map/ppermute | solution.py:244
  121.4 41.5 %collective-permute-start.17 = (bf16[512,1536]{1,0:T(8,128)(2,1)S(1)}, bf16[512,1536]{1,0:T(8,128)(2,1)}, u32[]{:S(2)}, u32[]{:S(2)}) collective-permute-start(bf16[512,1536]{1,0:T(8,128)(2,1)S(1)} %add.73.refs_15_), channel_id=1, source_target_pairs={{0,16},{16,0},{1,17},{17,1},{2,18},{18,2},{3,19},{19,3},{4,20},{20... | collective-permute-start | bytes 4718600 | tf_op jit(solution)/shard_map/ppermute | solution.py:247
  124.7 43.6 %collective-permute-start.19 = (bf16[1024,640]{1,0:T(8,128)(2,1)S(1)}, bf16[1024,640]{1,0:T(8,128)(2,1)S(1)}, u32[]{:S(2)}, u32[]{:S(2)}) collective-permute-start(bf16[1024,640]{1,0:T(8,128)(2,1)S(1)} %fusion.2), channel_id=1, source_target_pairs={{1,2},{2,1},{5,6},{6,5},{9,10},{10,9},{13,14},{14,13},{17,18},{18,... | collective-permute-start | bytes 3932168 | tf_op jit(solution)/shard_map/ppermute | solution.py:244
  133.7 89.1 %collective-permute-start.24 = (bf16[2,1024,512]{2,1,0:T(8,128)(2,1)}, bf16[2,1024,512]{2,1,0:T(8,128)(2,1)}, u32[]{:S(2)}, u32[]{:S(2)}) collective-permute-start(bf16[2,1024,512]{2,1,0:T(8,128)(2,1)} %get-tuple-element.71), channel_id=1, source_target_pairs={{0,1},{3,2},{4,5},{7,6},{8,9},{11,10},{12,13},{15,14},{16,17},{19,... | collective-permute-start | bytes 6291464 | tf_op jit(solution)/shard_map/ppermute | solution.py:244
  158.4 35.7 %collective-permute-start.20 = (bf16[1024,640]{1,0:T(8,128)(2,1)}, bf16[1024,640]{1,0:T(8,128)(2,1)}, u32[]{:S(2)}, u32[]{:S(2)}) collective-permute-start(bf16[1024,640]{1,0:T(8,128)(2,1)} %add_convert_fusion.1), channel_id=1, source_target_pairs={{1,0},{2,3},{5,4},{6,7},{9,8},{10,11},{13,12},{14,15},{17,16},{18,... | collective-permute-start | bytes 3932168 | tf_op jit(solution)/shard_map/ppermute | solution.py:244
  162.9 49.6 %collective-permute-start.22 = (bf16[512,1536]{1,0:T(8,128)(2,1)}, bf16[512,1536]{1,0:T(8,128)(2,1)}, u32[]{:S(2)}, u32[]{:S(2)}) collective-permute-start(bf16[512,1536]{1,0:T(8,128)(2,1)} %add.76.refs_13_), channel_id=1, source_target_pairs={{0,16},{16,0},{1,17},{17,1},{2,18},{18,2},{3,19},{19,3},{4,20},{20... | collective-permute-start | bytes 4718600 | tf_op jit(solution)/shard_map/ppermute | solution.py:247
  166.7 43.5 %collective-permute-start.21 = (bf16[1024,384]{1,0:T(8,128)(2,1)}, bf16[1024,384]{1,0:T(8,128)(2,1)}, u32[]{:S(2)}, u32[]{:S(2)}) collective-permute-start(bf16[1024,384]{1,0:T(8,128)(2,1)} %fusion.6), channel_id=1, source_target_pairs={{1,2},{2,1},{5,6},{6,5},{9,10},{10,9},{13,14},{14,13},{17,18},{18,... | collective-permute-start | bytes 2359304 | tf_op jit(solution)/shard_map/ppermute | solution.py:244
  171.7 51.1 %collective-permute-start.23 = (bf16[1024,384]{1,0:T(8,128)(2,1)}, bf16[1024,384]{1,0:T(8,128)(2,1)}, u32[]{:S(2)}, u32[]{:S(2)}) collective-permute-start(bf16[1024,384]{1,0:T(8,128)(2,1)} %fusion.7), channel_id=1, source_target_pairs={{1,2},{2,1},{5,6},{6,5},{9,10},{10,9},{13,14},{14,13},{17,18},{18,... | collective-permute-start | bytes 2359304 | tf_op jit(solution)/shard_map/ppermute | solution.py:244
  194.2 51.8 %collective-permute-start.25 = (bf16[1024,640]{1,0:T(8,128)(2,1)S(1)}, bf16[1024,640]{1,0:T(8,128)(2,1)S(1)}, u32[]{:S(2)}, u32[]{:S(2)}) collective-permute-start(bf16[1024,640]{1,0:T(8,128)(2,1)S(1)} %bitcast.28), channel_id=1, source_target_pairs={{0,1},{3,2},{4,5},{7,6},{8,9},{11,10},{12,13},{15,14},{16,17},{19,... | collective-permute-start | bytes 3932168 | tf_op jit(solution)/shard_map/ppermute | solution.py:244
  224.5 21.5 %collective-permute-start.27 = (bf16[1024,512]{1,0:T(8,128)(2,1)S(1)}, bf16[1024,512]{1,0:T(8,128)(2,1)S(1)}, u32[]{:S(2)}, u32[]{:S(2)}) collective-permute-start(bf16[1024,512]{1,0:T(8,128)(2,1)S(1)} %fusion.3), channel_id=1, source_target_pairs={{1,2},{2,1},{5,6},{6,5},{9,10},{10,9},{13,14},{14,13},{17,18},{18,... | collective-permute-start | bytes 3145736 | tf_op jit(solution)/shard_map/ppermute | solution.py:244
  226.7 37.7 %collective-permute-start.30 = (bf16[1024,512]{1,0:T(8,128)(2,1)S(1)}, bf16[1024,512]{1,0:T(8,128)(2,1)S(1)}, u32[]{:S(2)}, u32[]{:S(2)}) collective-permute-start(bf16[1024,512]{1,0:T(8,128)(2,1)S(1)} %bitcast.29), channel_id=1, source_target_pairs={{0,1},{3,2},{4,5},{7,6},{8,9},{11,10},{12,13},{15,14},{16,17},{19,... | collective-permute-start | bytes 3145736 | tf_op jit(solution)/shard_map/ppermute | solution.py:244
  232.9 31.4 %collective-permute-start.28 = (bf16[1024,512]{1,0:T(8,128)(2,1)S(1)}, bf16[1024,512]{1,0:T(8,128)(2,1)S(1)}, u32[]{:S(2)}, u32[]{:S(2)}) collective-permute-start(bf16[1024,512]{1,0:T(8,128)(2,1)S(1)} %fusion.4), channel_id=1, source_target_pairs={{1,2},{2,1},{5,6},{6,5},{9,10},{10,9},{13,14},{14,13},{17,18},{18,... | collective-permute-start | bytes 3145736 | tf_op jit(solution)/shard_map/ppermute | solution.py:244
  246.3 26.9 %collective-permute-start.29 = (bf16[1024,512]{1,0:T(8,128)(2,1)S(1)}, bf16[1024,512]{1,0:T(8,128)(2,1)S(1)}, u32[]{:S(2)}, u32[]{:S(2)}) collective-permute-start(bf16[1024,512]{1,0:T(8,128)(2,1)S(1)} %add_convert_fusion.5), channel_id=1, source_target_pairs={{1,0},{2,3},{5,4},{6,7},{9,8},{10,11},{13,12},{14,15},{17,16},{18,... | collective-permute-start | bytes 3145736 | tf_op jit(solution)/shard_map/ppermute | solution.py:244
  (44 other events, 666.2 us)

commit v4 on v3

--- a/solution.py
+++ b/solution.py
@@ -371,8 +371,8 @@
     send_middle(1, 1, middle_sums[1])
     near_weights = [first, first_far, second, second_far]
     attended_gradient((1, 2), out_weight, near_weights, jnp.float32)
+    attended_gradient((3,), grad_att[0], [third, third_far], jnp.bfloat16)
     send_outward(1, outward_sums[0])
-    attended_gradient((3,), grad_att[0], [third, third_far], jnp.bfloat16)
     send_middle(0, 2, middle_sums[3])
     send_middle(1, 2)
     backward(0)

time: 277 us -> 271 us (0.978)
  starting transfers between devices: 81 us -> 73.4 us
    ppermute x19, waiting for transfers between devices: 15.7 us -> 31.1 us  [along(): return lax.ppermute(array, 'dp', pairs)]
    ppermute x3, waiting for transfers between devices: 37.9 us -> 24 us  [gather(): across = lax.ppermute(mine, 'mp', [(i, i ^ 2) for i in range(4)])]
    ppermute x19, starting transfers between devices: 70 us -> 62.5 us  [along(): return lax.ppermute(array, 'dp', pairs)]
    unnamed x74 -> x72, local copies, waits for them, and re-layouts: 9.31 us -> 8.38 us
  transfers between devices with their start and end apart: 31 -> 31, of which waited for: 6 -> 8; matrix products, arithmetic and copies ran while one was open for 11% -> 12% of each run, Pallas kernels for 34% -> 34%
where the time goes in v4:
time: 271 us; the launch traced here: 270 us
  Pallas kernels  93 us (34%)
  starting transfers between devices  73.4 us (27%)
  waiting for transfers between devices  59.3 us (22%)
  other arithmetic  31.5 us (12%)
  local copies, waits for them, and re-layouts  11.8 us (4%)
    ppermute x19, starting transfers between devices, along(): return lax.ppermute(array, 'dp', pairs)  62.5 us
    ppermute x19, waiting for transfers between devices, along(): return lax.ppermute(array, 'dp', pairs)  31.1 us
    pallas_call x3, Pallas kernels, partial_call(): pl.pallas_call(partial_kernel, grid_spec=pltpu.PrefetchScalarGridSpec(num...  27.6 us
    pallas_call x2, Pallas kernels, attended_call(): pl.pallas_call(functools.partial(attended_kernel, blocks, slots), grid_sp...  27.6 us
    pallas_call x2, Pallas kernels, attention_backward(): pl.pallas_call(backward_kernel, grid=(rows // LEN, width // block), in_sp...  24.5 us
    ppermute x3, waiting for transfers between devices, gather(): across = lax.ppermute(mine, 'mp', [(i, i ^ 2) for i in range(4)])  24 us
    pallas_call x1, Pallas kernels, attention_forward(): pl.pallas_call(forward_kernel, grid=(tokens // LEN, width // block), in_s...  13.3 us
    convert_element_type x6, other arithmetic, send_middle(): middle_sums.append(along(done(value.astype(jnp.bfloat16)), MIDDLE))  13 us
  transfers between devices with their start and end apart: 31, of which 8 were waited for; matrix products, arithmetic and copies ran while one was open for 12% of the time, Pallas kernels for 34%

profile of v4, /device:TPU:0, one launch (start us, length us, event | category | flops | bytes accessed | tf_op | source)
XLA Modules:
  0.0 270.1 jit_solution(17771069030785310161)
XLA Ops:
  0.6 3.2 %convert.6 = bf16[1024,1536]{1,0:T(8,128)(2,1)S(1)} convert(f32[1024,1536]{1,0:T(8,128)} %param.5) | non-fusion elementwise | flops 1572864 | bytes 9437184 | tf_op jit(solution)/shard_map/convert.3
  5.6 3.0 %collective-permute-start.1 = (bf16[1024,640]{1,0:T(8,128)(2,1)S(1)}, bf16[1024,640]{1,0:T(8,128)(2,1)S(1)}, u32[]{:S(2)}, u32[]{:S(2)}) collective-permute-start(bf16[1024,640]{1,0:T(8,128)(2,1)S(1)} %slice.67.refs_0_), channel_id=1, source_target_pairs={{0,8},{4,12},{8,0},{12,4},{1,9},{5,13},{9,1},{13,5},{2,10},{6,14},... | collective-permute-start | bytes 3932168 | tf_op jit(solution)/shard_map/ppermute | solution.py:282
  14.9 13.3 %shard_map.59.attended = bf16[1024,1024]{1,0:T(8,128)(2,1)S(1)} custom-call(s32[2,512,1]{2,1,0:T(8,128)S(1)} %copy.9.column_ids, s32[2,1,512]{2,1,0:T(1,128)S(1)} %reshape.41.row_ids, bf16[3,1024,1024]{2,1,0:T(8,128)(2,1)} %qkv.5), custom_call_target="tpu_custom_call" | custom-call | flops 107374184 | bytes 419430 | tf_op jit(solution)/shard_map/pallas_call | solution.py:81
  29.4 8.0 %collective-permute-done.1.refs_2_.refs_6_ = bf16[1024,640]{1,0:T(8,128)(2,1)S(1)} collective-permute-done((bf16[1024,640]{1,0:T(8,128)(2,1)S(1)}, bf16[1024,640]{1,0:T(8,128)(2,1)S(1)}, u32[]{:S(2)}, u32[]{:S(2)}) %collective-permute-start.1) | collective-permute-done | bytes 1310752 | tf_op jit(solution)/shard_map/ppermute | solution.py:282
  37.5 3.1 %collective-permute-done.2.refs_3_.refs_9_ = bf16[1024,640]{1,0:T(8,128)(2,1)} collective-permute-done((bf16[1024,640]{1,0:T(8,128)(2,1)S(1)}, bf16[1024,640]{1,0:T(8,128)(2,1)}, u32[]{:S(2)}, u32[]{:S(2)}) %collective-permute-start.2) | collective-permute-done | bytes 1310752 | tf_op jit(solution)/shard_map/ppermute | solution.py:283
  40.6 11.5 %shard_map.60 = (bf16[2,1024,640]{2,1,0:T(8,128)(2,1)}, bf16[1,1024,640]{2,1,0:T(8,128)(2,1)S(1)}, f32[1024,640]{1,0:T(8,128)}) custom-call(s32[4]{0:T(128)S(1)} %pad_add_fusion.order, bf16[1024,1024]{1,0:T(8,128)(2,1)} %copy-done, bf16[1024,640]{1,0:T(8,128)(2,1)S(1)} %slice.67.refs_0_, bf16[1024,640]{1,0:T(8,128)(2,1)} %collective-permute-done.refs_1_.refs_3_, ...), custom_call_target="tpu_custom_call" | custom-call | flops 268435456 | bytes 629145 | tf_op jit(solution)/shard_map/pallas_call | solution.py:129
  52.1 5.2 %collective-permute-start.9 = (bf16[2,1024,640]{2,1,0:T(8,128)(2,1)}, bf16[2,1024,640]{2,1,0:T(8,128)(2,1)}, u32[]{:S(2)}, u32[]{:S(2)}) collective-permute-start(bf16[2,1024,640]{2,1,0:T(8,128)(2,1)} %get-tuple-element.54), channel_id=1, source_target_pairs={{0,1},{3,2},{4,5},{7,6},{8,9},{11,10},{12,13},{15,14},{16,17},{19,... | collective-permute-start | bytes 7864328 | tf_op jit(solution)/shard_map/ppermute | solution.py:244
  60.8 16.0 %collective-permute-done.6.refs_2_.refs_7_ = bf16[1024,384]{1,0:T(8,128)(2,1)S(1)} collective-permute-done((bf16[1024,384]{1,0:T(8,128)(2,1)S(1)}, bf16[1024,384]{1,0:T(8,128)(2,1)S(1)}, u32[]{:S(2)}, u32[]{:S(2)}) %collective-permute-start.6) | collective-permute-done | bytes 786464 | tf_op jit(solution)/shard_map/ppermute | solution.py:282
  81.3 8.0 %shard_map.61 = (bf16[3,1024,384]{2,1,0:T(8,128)(2,1)}, bf16[1,1024,384]{2,1,0:T(8,128)(2,1)S(1)}, f32[1024,384]{1,0:T(8,128)S(1)}) custom-call(s32[4]{0:T(128)S(1)} %pad_add_fusion.order, bf16[1024,1024]{1,0:T(8,128)(2,1)} %copy-done, bf16[1024,384]{1,0:T(8,128)(2,1)S(1)} %slice.68.refs_0_.refs_1_, ...), custom_call_target="tpu_custom_call" | custom-call | flops 161061280 | bytes 419430 | tf_op jit(solution)/shard_map/pallas_call | solution.py:129
  89.4 23.2 %collective-permute-done.9 = bf16[2,1024,640]{2,1,0:T(8,128)(2,1)} collective-permute-done((bf16[2,1024,640]{2,1,0:T(8,128)(2,1)}, bf16[2,1024,640]{2,1,0:T(8,128)(2,1)}, u32[]{:S(2)}, u32[]{:S(2)}) %collective-permute-start.9) | collective-permute-done | bytes 2621472 | tf_op jit(solution)/shard_map/ppermute | solution.py:244
  112.5 5.8 %collective-permute-start.18 = (bf16[3,1024,384]{2,1,0:T(8,128)(2,1)}, bf16[3,1024,384]{2,1,0:T(8,128)(2,1)}, u32[]{:S(2)}, u32[]{:S(2)}) collective-permute-start(bf16[3,1024,384]{2,1,0:T(8,128)(2,1)} %get-tuple-element.62), channel_id=1, source_target_pairs={{0,1},{3,2},{4,5},{7,6},{8,9},{11,10},{12,13},{15,14},{16,17},{19,... | collective-permute-start | bytes 7077896 | tf_op jit(solution)/shard_map/ppermute | solution.py:244
  118.4 2.7 %fusion.1 = bf16[1024,640]{1,0:T(8,128)(2,1)} fusion(bf16[2,1024,640]{2,1,0:T(8,128)(2,1)} %collective-permute-done.9, bf16[2,1024,640]{2,1,0:T(8,128)(2,1)S(1)} %copy-done.29), kind=kLoop, calls=%fused_computation.13 | loop fusion | flops 2621440 | bytes 3932160 | tf_op jit(solution)/shard_map/convert_element_type | solution.py:305
  128.2 2.8 %fusion.2 = bf16[1024,640]{1,0:T(8,128)(2,1)} fusion(bf16[2,1024,640]{2,1,0:T(8,128)(2,1)} %collective-permute-done.9, bf16[2,1024,640]{2,1,0:T(8,128)(2,1)S(1)} %copy-done.29), kind=kLoop, calls=%fused_computation.14 | loop fusion | flops 2621440 | bytes 3932160 | tf_op jit(solution)/shard_map/convert_element_type | solution.py:305
  132.7 8.1 %shard_map.62 = (bf16[2,1024,512]{2,1,0:T(8,128)(2,1)}, bf16[1,1024,512]{2,1,0:T(8,128)(2,1)S(1)}, f32[1024,512]{1,0:T(8,128)}) custom-call(s32[4]{0:T(128)S(1)} %pad_add_fusion.order, bf16[1024,1024]{1,0:T(8,128)(2,1)} %copy-done, bf16[1024,512]{1,0:T(8,128)(2,1)S(1)} %slice.71.refs_0_.refs_2_, ...), custom_call_target="tpu_custom_call" | custom-call | flops 214748368 | bytes 524288 | tf_op jit(solution)/shard_map/pallas_call | solution.py:129
  140.9 15.4 %collective-permute-start.24 = (bf16[2,1024,512]{2,1,0:T(8,128)(2,1)}, bf16[2,1024,512]{2,1,0:T(8,128)(2,1)}, u32[]{:S(2)}, u32[]{:S(2)}) collective-permute-start(bf16[2,1024,512]{2,1,0:T(8,128)(2,1)} %get-tuple-element.71), channel_id=1, source_target_pairs={{0,1},{3,2},{4,5},{7,6},{8,9},{11,10},{12,13},{15,14},{16,17},{19,... | collective-permute-start | bytes 6291464 | tf_op jit(solution)/shard_map/ppermute | solution.py:244
  156.3 2.7 %add_convert_fusion.1 = bf16[1024,640]{1,0:T(8,128)(2,1)} fusion(bf16[1024,640]{1,0:T(8,128)(2,1)} %collective-permute-done.15, bf16[1024,640]{1,0:T(8,128)(2,1)S(1)} %bitcast.27), kind=kLoop, calls=%fused_computation.1 | loop fusion | flops 2621440 | bytes 3932160 | tf_op jit(solution)/shard_map/convert_element_type | solution.py:311
  160.4 3.4 %add.76.refs_13_ = bf16[512,1536]{1,0:T(8,128)(2,1)} add(bf16[512,1536]{1,0:T(8,128)(2,1)} %collective-permute-done.4, bf16[512,1536]{1,0:T(8,128)(2,1)} %collective-permute-done.16) | non-fusion elementwise | flops 786432 | bytes 4718592 | tf_op jit(solution)/shard_map/add | solution.py:367
  180.0 17.4 %shard_map.63.refs_12_ = f32[1024,1024]{1,0:T(8,128)} custom-call(s32[5]{0:T(128)S(1)} %stack.32.order, bf16[1024,640]{1,0:T(8,128)(2,1)} %copy-done.1, bf16[1024,384]{1,0:T(8,128)(2,1)S(1)} %slice.68.refs_0_.refs_1_, bf16[1024,512]{1,0:T(8,128)(2,1)S(1)} %slice.71.refs_0_.refs_2_, bf16[1024,640]{1,0:T(8,128)(2,1)} %collective-permute-done.refs_1_.refs_3_, ...), custom_call_target="tpu_custom_call" | custom-call | flops 322122560 | bytes 1468006 | tf_op jit(solution)/shard_map/pallas_call | solution.py:196
  198.6 11.4 %collective-permute-start.25 = (bf16[1024,640]{1,0:T(8,128)(2,1)S(1)}, bf16[1024,640]{1,0:T(8,128)(2,1)S(1)}, u32[]{:S(2)}, u32[]{:S(2)}) collective-permute-start(bf16[1024,640]{1,0:T(8,128)(2,1)S(1)} %bitcast.28), channel_id=1, source_target_pairs={{0,1},{3,2},{4,5},{7,6},{8,9},{11,10},{12,13},{15,14},{16,17},{19,... | collective-permute-start | bytes 3932168 | tf_op jit(solution)/shard_map/ppermute | solution.py:244
  210.0 10.2 %shard_map.64.grad_att = bf16[1024,1024]{1,0:T(8,128)(2,1)} custom-call(s32[5]{0:T(128)S(1)} %stack.32.order, bf16[1024,640]{1,0:T(8,128)(2,1)} %copy-done.1, bf16[1024,384]{1,0:T(8,128)(2,1)S(1)} %slice.68.refs_0_.refs_1_, bf16[1024,512]{1,0:T(8,128)(2,1)S(1)} %slice.71.refs_0_.refs_2_, bf16[1024,640]{1,0:T(8,128)(2,1)} %collective-permute-done.refs_1_.refs_3_, ...), custom_call_target="tpu_custom_call" | custom-call | flops 161061280 | bytes 1468006 | tf_op jit(solution)/shard_map/pallas_call | solution.py:196
  225.8 4.7 %collective-permute-start.30 = (bf16[1024,512]{1,0:T(8,128)(2,1)S(1)}, bf16[1024,512]{1,0:T(8,128)(2,1)S(1)}, u32[]{:S(2)}, u32[]{:S(2)}) collective-permute-start(bf16[1024,512]{1,0:T(8,128)(2,1)S(1)} %bitcast.29), channel_id=1, source_target_pairs={{0,1},{3,2},{4,5},{7,6},{8,9},{11,10},{12,13},{15,14},{16,17},{19,... | collective-permute-start | bytes 3145736 | tf_op jit(solution)/shard_map/ppermute | solution.py:244
  232.7 12.2 %shard_map.65.refs_0_ = bf16[3,1024,1024]{2,1,0:T(8,128)(2,1)} custom-call(s32[2,512,1]{2,1,0:T(8,128)S(1)} %copy-done.9, s32[2,1,512]{2,1,0:T(1,128)S(1)} %reshape.41.row_ids, bf16[3,1024,1024]{2,1,0:T(8,128)(2,1)} %qkv.5, bf16[1024,1024]{1,0:T(8,128)(2,1)S(1)} %copy-done.2), custom_call_target="tpu_custom_call" | custom-call | flops 134217728 | bytes 367001 | tf_op jit(solution)/shard_map/pallas_call | solution.py:102
  249.3 12.3 %shard_map.66 = bf16[3,1024,1024]{2,1,0:T(8,128)(2,1)} custom-call(s32[2,512,1]{2,1,0:T(8,128)S(1)} %copy-done.9, s32[2,1,512]{2,1,0:T(1,128)S(1)} %reshape.41.row_ids, bf16[3,1024,1024]{2,1,0:T(8,128)(2,1)} %qkv.5, bf16[1024,1024]{1,0:T(8,128)(2,1)S(1)} %copy-done.2, bf16[3,1024,1024]{2,1,0:T(8,128)(2,1)} %shard_map.65.refs_0_), custom_call_target="tpu_custom_call", output_to_operand_aliasing={{}: (4, {})} | custom-call | flops 134217728 | bytes 367001 | tf_op jit(solution)/shard_map/pallas_call | solution.py:102
  263.7 4.2 %collective-permute-done.29 = bf16[1024,512]{1,0:T(8,128)(2,1)S(1)} collective-permute-done((bf16[1024,512]{1,0:T(8,128)(2,1)S(1)}, bf16[1024,512]{1,0:T(8,128)(2,1)S(1)}, u32[]{:S(2)}, u32[]{:S(2)}) %collective-permute-start.29) | collective-permute-done | bytes 1048608 | tf_op jit(solution)/shard_map/ppermute | solution.py:244
  (142 shorter events, 61.3 us)
Async XLA Ops:
  5.6 31.8 %collective-permute-start.1 = (bf16[1024,640]{1,0:T(8,128)(2,1)S(1)}, bf16[1024,640]{1,0:T(8,128)(2,1)S(1)}, u32[]{:S(2)}, u32[]{:S(2)}) collective-permute-start(bf16[1024,640]{1,0:T(8,128)(2,1)S(1)} %slice.67.refs_0_), channel_id=1, source_target_pairs={{0,8},{4,12},{8,0},{12,4},{1,9},{5,13},{9,1},{13,5},{2,10},{6,14},... | collective-permute-start | bytes 3932168 | tf_op jit(solution)/shard_map/ppermute | solution.py:282
  11.2 40.8 %collective-permute-start.3 = (bf16[512,1536]{1,0:T(8,128)(2,1)}, bf16[512,1536]{1,0:T(8,128)(2,1)}, u32[]{:S(2)}, u32[]{:S(2)}) collective-permute-start(bf16[512,1536]{1,0:T(8,128)(2,1)} %constant_dynamic-slice_fusion), channel_id=1, source_target_pairs={{0,1},{1,0},{2,3},{3,2},{4,5},{5,4},{6,7},{7,6},{8,9},{9,8},{10,11... | collective-permute-start | bytes 4718600 | tf_op jit(solution)/shard_map/ppermute | solution.py:244
  12.8 39.2 %collective-permute-start.8 = (bf16[512,1536]{1,0:T(8,128)(2,1)}, bf16[512,1536]{1,0:T(8,128)(2,1)}, u32[]{:S(2)}, u32[]{:S(2)}) collective-permute-start(bf16[512,1536]{1,0:T(8,128)(2,1)} %constant_dynamic-slice_fusion), channel_id=1, source_target_pairs={{1,2},{2,1},{5,6},{6,5},{9,10},{10,9},{13,14},{14,13},{17,18},{18,... | collective-permute-start | bytes 4718600 | tf_op jit(solution)/shard_map/ppermute | solution.py:244
  14.6 22.9 %collective-permute-start = (bf16[1024,640]{1,0:T(8,128)(2,1)S(1)}, bf16[1024,640]{1,0:T(8,128)(2,1)}, u32[]{:S(2)}, u32[]{:S(2)}) collective-permute-start(bf16[1024,640]{1,0:T(8,128)(2,1)S(1)} %slice.67.refs_0_), channel_id=1, source_target_pairs={{0,4},{4,0},{8,12},{12,8},{1,5},{5,1},{9,13},{13,9},{2,6},{6,2},{1... | collective-permute-start | bytes 3932168 | tf_op jit(solution)/shard_map/ppermute | solution.py:281
  52.1 60.5 %collective-permute-start.9 = (bf16[2,1024,640]{2,1,0:T(8,128)(2,1)}, bf16[2,1024,640]{2,1,0:T(8,128)(2,1)}, u32[]{:S(2)}, u32[]{:S(2)}) collective-permute-start(bf16[2,1024,640]{2,1,0:T(8,128)(2,1)} %get-tuple-element.54), channel_id=1, source_target_pairs={{0,1},{3,2},{4,5},{7,6},{8,9},{11,10},{12,13},{15,14},{16,17},{19,... | collective-permute-start | bytes 7864328 | tf_op jit(solution)/shard_map/ppermute | solution.py:244
  59.0 22.4 %collective-permute-start.4 = (bf16[512,1536]{1,0:T(8,128)(2,1)}, bf16[512,1536]{1,0:T(8,128)(2,1)}, u32[]{:S(2)}, u32[]{:S(2)}) collective-permute-start(bf16[512,1536]{1,0:T(8,128)(2,1)} %collective-permute-done.3.refs_13_), channel_id=1, source_target_pairs={{1,2},{2,1},{5,6},{6,5},{9,10},{10,9},{13,14},{14,13},{17,18},{18,... | collective-permute-start | bytes 4718600 | tf_op jit(solution)/shard_map/ppermute | solution.py:244
  76.8 47.4 %collective-permute-start.10 = (bf16[512,1536]{1,0:T(8,128)(2,1)}, bf16[512,1536]{1,0:T(8,128)(2,1)}, u32[]{:S(2)}, u32[]{:S(2)}) collective-permute-start(bf16[512,1536]{1,0:T(8,128)(2,1)} %collective-permute-done.8), channel_id=1, source_target_pairs={{1,0},{2,3},{5,4},{6,7},{9,8},{10,11},{13,12},{14,15},{17,16},{18,... | collective-permute-start | bytes 4718600 | tf_op jit(solution)/shard_map/ppermute | solution.py:244
  78.1 48.5 %collective-permute-start.11 = (bf16[512,1536]{1,0:T(8,128)(2,1)}, bf16[512,1536]{1,0:T(8,128)(2,1)S(1)}, u32[]{:S(2)}, u32[]{:S(2)}) collective-permute-start(bf16[512,1536]{1,0:T(8,128)(2,1)} %collective-permute-done.3.refs_13_), channel_id=1, source_target_pairs={{0,16},{16,0},{1,17},{17,1},{2,18},{18,2},{3,19},{19,3},{4,20},{20... | collective-permute-start | bytes 4718600 | tf_op jit(solution)/shard_map/ppermute | solution.py:247
  79.8 41.3 %collective-permute-start.13 = (bf16[1024,512]{1,0:T(8,128)(2,1)S(1)}, bf16[1024,512]{1,0:T(8,128)(2,1)S(1)}, u32[]{:S(2)}, u32[]{:S(2)}) collective-permute-start(bf16[1024,512]{1,0:T(8,128)(2,1)S(1)} %slice.71.refs_0_.refs_2_), channel_id=1, source_target_pairs={{0,8},{4,12},{8,0},{12,4},{1,9},{5,13},{9,1},{13,5},{2,10},{6,14},... | collective-permute-start | bytes 3145736 | tf_op jit(solution)/shard_map/ppermute | solution.py:282
  81.3 41.6 %collective-permute-start.12 = (bf16[1024,512]{1,0:T(8,128)(2,1)S(1)}, bf16[1024,512]{1,0:T(8,128)(2,1)S(1)}, u32[]{:S(2)}, u32[]{:S(2)}) collective-permute-start(bf16[1024,512]{1,0:T(8,128)(2,1)S(1)} %slice.71.refs_0_.refs_2_), channel_id=1, source_target_pairs={{0,4},{4,0},{8,12},{12,8},{1,5},{5,1},{9,13},{13,9},{2,6},{6,2},{1... | collective-permute-start | bytes 3145736 | tf_op jit(solution)/shard_map/ppermute | solution.py:281
  112.5 56.4 %collective-permute-start.18 = (bf16[3,1024,384]{2,1,0:T(8,128)(2,1)}, bf16[3,1024,384]{2,1,0:T(8,128)(2,1)}, u32[]{:S(2)}, u32[]{:S(2)}) collective-permute-start(bf16[3,1024,384]{2,1,0:T(8,128)(2,1)} %get-tuple-element.62), channel_id=1, source_target_pairs={{0,1},{3,2},{4,5},{7,6},{8,9},{11,10},{12,13},{15,14},{16,17},{19,... | collective-permute-start | bytes 7077896 | tf_op jit(solution)/shard_map/ppermute | solution.py:244
  122.9 37.5 %collective-permute-start.16 = (bf16[512,1536]{1,0:T(8,128)(2,1)}, bf16[512,1536]{1,0:T(8,128)(2,1)}, u32[]{:S(2)}, u32[]{:S(2)}) collective-permute-start(bf16[512,1536]{1,0:T(8,128)(2,1)} %collective-permute-done.4), channel_id=1, source_target_pairs={{1,0},{2,3},{5,4},{6,7},{9,8},{10,11},{13,12},{14,15},{17,16},{18,... | collective-permute-start | bytes 4718600 | tf_op jit(solution)/shard_map/ppermute | solution.py:244
  126.6 38.7 %collective-permute-start.17 = (bf16[512,1536]{1,0:T(8,128)(2,1)S(1)}, bf16[512,1536]{1,0:T(8,128)(2,1)S(1)}, u32[]{:S(2)}, u32[]{:S(2)}) collective-permute-start(bf16[512,1536]{1,0:T(8,128)(2,1)S(1)} %add.73.refs_15_), channel_id=1, source_target_pairs={{0,16},{16,0},{1,17},{17,1},{2,18},{18,2},{3,19},{19,3},{4,20},{20... | collective-permute-start | bytes 4718600 | tf_op jit(solution)/shard_map/ppermute | solution.py:247
  131.0 41.8 %collective-permute-start.19 = (bf16[1024,640]{1,0:T(8,128)(2,1)}, bf16[1024,640]{1,0:T(8,128)(2,1)}, u32[]{:S(2)}, u32[]{:S(2)}) collective-permute-start(bf16[1024,640]{1,0:T(8,128)(2,1)} %fusion.2), channel_id=1, source_target_pairs={{1,2},{2,1},{5,6},{6,5},{9,10},{10,9},{13,14},{14,13},{17,18},{18,... | collective-permute-start | bytes 3932168 | tf_op jit(solution)/shard_map/ppermute | solution.py:244
  140.9 80.9 %collective-permute-start.24 = (bf16[2,1024,512]{2,1,0:T(8,128)(2,1)}, bf16[2,1024,512]{2,1,0:T(8,128)(2,1)}, u32[]{:S(2)}, u32[]{:S(2)}) collective-permute-start(bf16[2,1024,512]{2,1,0:T(8,128)(2,1)} %get-tuple-element.71), channel_id=1, source_target_pairs={{0,1},{3,2},{4,5},{7,6},{8,9},{11,10},{12,13},{15,14},{16,17},{19,... | collective-permute-start | bytes 6291464 | tf_op jit(solution)/shard_map/ppermute | solution.py:244
  163.8 34.7 %collective-permute-start.20 = (bf16[512,1536]{1,0:T(8,128)(2,1)}, bf16[512,1536]{1,0:T(8,128)(2,1)}, u32[]{:S(2)}, u32[]{:S(2)}) collective-permute-start(bf16[512,1536]{1,0:T(8,128)(2,1)} %add.76.refs_13_), channel_id=1, source_target_pairs={{0,16},{16,0},{1,17},{17,1},{2,18},{18,2},{3,19},{19,3},{4,20},{20... | collective-permute-start | bytes 4718600 | tf_op jit(solution)/shard_map/ppermute | solution.py:247
  165.4 54.9 %collective-permute-start.21 = (bf16[1024,640]{1,0:T(8,128)(2,1)}, bf16[1024,640]{1,0:T(8,128)(2,1)}, u32[]{:S(2)}, u32[]{:S(2)}) collective-permute-start(bf16[1024,640]{1,0:T(8,128)(2,1)} %add_convert_fusion.1), channel_id=1, source_target_pairs={{1,0},{2,3},{5,4},{6,7},{9,8},{10,11},{13,12},{14,15},{17,16},{18,... | collective-permute-start | bytes 3932168 | tf_op jit(solution)/shard_map/ppermute | solution.py:244
  171.2 49.0 %collective-permute-start.22 = (bf16[1024,384]{1,0:T(8,128)(2,1)}, bf16[1024,384]{1,0:T(8,128)(2,1)}, u32[]{:S(2)}, u32[]{:S(2)}) collective-permute-start(bf16[1024,384]{1,0:T(8,128)(2,1)} %fusion.6), channel_id=1, source_target_pairs={{1,2},{2,1},{5,6},{6,5},{9,10},{10,9},{13,14},{14,13},{17,18},{18,... | collective-permute-start | bytes 2359304 | tf_op jit(solution)/shard_map/ppermute | solution.py:244
  175.0 46.8 %collective-permute-start.23 = (bf16[1024,384]{1,0:T(8,128)(2,1)}, bf16[1024,384]{1,0:T(8,128)(2,1)}, u32[]{:S(2)}, u32[]{:S(2)}) collective-permute-start(bf16[1024,384]{1,0:T(8,128)(2,1)} %fusion.7), channel_id=1, source_target_pairs={{1,2},{2,1},{5,6},{6,5},{9,10},{10,9},{13,14},{14,13},{17,18},{18,... | collective-permute-start | bytes 2359304 | tf_op jit(solution)/shard_map/ppermute | solution.py:244
  198.6 46.3 %collective-permute-start.25 = (bf16[1024,640]{1,0:T(8,128)(2,1)S(1)}, bf16[1024,640]{1,0:T(8,128)(2,1)S(1)}, u32[]{:S(2)}, u32[]{:S(2)}) collective-permute-start(bf16[1024,640]{1,0:T(8,128)(2,1)S(1)} %bitcast.28), channel_id=1, source_target_pairs={{0,1},{3,2},{4,5},{7,6},{8,9},{11,10},{12,13},{15,14},{16,17},{19,... | collective-permute-start | bytes 3932168 | tf_op jit(solution)/shard_map/ppermute | solution.py:244
  223.6 21.3 %collective-permute-start.27 = (bf16[1024,512]{1,0:T(8,128)(2,1)S(1)}, bf16[1024,512]{1,0:T(8,128)(2,1)S(1)}, u32[]{:S(2)}, u32[]{:S(2)}) collective-permute-start(bf16[1024,512]{1,0:T(8,128)(2,1)S(1)} %fusion.3), channel_id=1, source_target_pairs={{1,2},{2,1},{5,6},{6,5},{9,10},{10,9},{13,14},{14,13},{17,18},{18,... | collective-permute-start | bytes 3145736 | tf_op jit(solution)/shard_map/ppermute | solution.py:244
  225.8 37.9 %collective-permute-start.30 = (bf16[1024,512]{1,0:T(8,128)(2,1)S(1)}, bf16[1024,512]{1,0:T(8,128)(2,1)S(1)}, u32[]{:S(2)}, u32[]{:S(2)}) collective-permute-start(bf16[1024,512]{1,0:T(8,128)(2,1)S(1)} %bitcast.29), channel_id=1, source_target_pairs={{0,1},{3,2},{4,5},{7,6},{8,9},{11,10},{12,13},{15,14},{16,17},{19,... | collective-permute-start | bytes 3145736 | tf_op jit(solution)/shard_map/ppermute | solution.py:244
  231.9 31.7 %collective-permute-start.28 = (bf16[1024,512]{1,0:T(8,128)(2,1)S(1)}, bf16[1024,512]{1,0:T(8,128)(2,1)S(1)}, u32[]{:S(2)}, u32[]{:S(2)}) collective-permute-start(bf16[1024,512]{1,0:T(8,128)(2,1)S(1)} %fusion.4), channel_id=1, source_target_pairs={{1,2},{2,1},{5,6},{6,5},{9,10},{10,9},{13,14},{14,13},{17,18},{18,... | collective-permute-start | bytes 3145736 | tf_op jit(solution)/shard_map/ppermute | solution.py:244
  245.2 22.6 %collective-permute-start.29 = (bf16[1024,512]{1,0:T(8,128)(2,1)S(1)}, bf16[1024,512]{1,0:T(8,128)(2,1)S(1)}, u32[]{:S(2)}, u32[]{:S(2)}) collective-permute-start(bf16[1024,512]{1,0:T(8,128)(2,1)S(1)} %add_convert_fusion.5), channel_id=1, source_target_pairs={{1,0},{2,3},{5,4},{6,7},{9,8},{10,11},{13,12},{14,15},{17,16},{18,... | collective-permute-start | bytes 3145736 | tf_op jit(solution)/shard_map/ppermute | solution.py:244
  (43 other events, 641.0 us)
